TPU v7x, 512 devices: a whole 4x4x16 slice. The times are simulated.
512 devices in a mesh: gx: 32 (over x_hi, z), gy: 16 (over y, x_lo, core).
Axes of the slice: x: 4 (x_hi: 2, x_lo: 2; x = x_hi * 2 + x_lo), y: 4, z: 16, core: 2. Of those that a mesh axis runs over, the one named last changes fastest.
Arguments:
- flow_pops: float32 [19, 192, 128, 128], P(None, 'gx', 'gy'), may hold values from 0 to 0.5, as said below
- warmth_distribution: float32 [7, 192, 128, 128], P(None, 'gx', 'gy'), may hold values from 0 to 0.65, as said below
- fill_mass: float32 [192, 128, 128], P('gx', 'gy'), may hold values from 0.1 to 1
- diffusivity: float32 [192, 128, 128], P('gx', 'gy'), may hold values from 0.02 to 0.3
- heat_source: float32 [192, 128, 128], P('gx', 'gy'), may hold values from 0 to 0.2
- cell_kind: int32 [192, 128, 128], P('gx', 'gy'), may hold values from 0 to 3, as said below
- fill_masks: int32 [2, 192, 128, 128], P(None, 'gx', 'gy'), may hold values from 0 to 511
Outputs:
- flow_out: float32 [19, 192, 128, 128], P(None, 'gx', 'gy')
- heat_out: float32 [7, 192, 128, 128], P(None, 'gx', 'gy')
- mass_out: float32 [192, 128, 128], P('gx', 'gy')
Inputs may be any that keep to these rules, and one draw needn't show every extreme that they name: `cell_kind`: outermost cells in x and y and the bottom layer in z are walls; each column holds liquid below gas, with its surface at any height; a non-wall non-gas cell is interface exactly when one of its 18 neighbours is gas. `flow_pops`: each population is its lattice weight times a factor in 0.5 to 1.5. `warmth_distribution`: each population is its lattice weight times a positive temperature-like factor.
All inputs are finite; a program needn't handle non-finite values.
Results may differ from a plain program's by a relative error of at most 0.0003.
Values sent between devices are 32-bit elements; how exact they have to be, the bound alone decides.
A program may use at most 64 MiB of HBM per device.

v0:
```python
import jax
import jax.numpy as jnp
import numpy as np
from jax import lax
from jax.sharding import PartitionSpec as P

ITERS = 3


VELOCITY = [
    (0, 0, 0),
    (1, 0, 0),
    (-1, 0, 0),
    (0, 1, 0),
    (0, -1, 0),
    (0, 0, 1),
    (0, 0, -1),
    (1, 1, 0),
    (-1, -1, 0),
    (1, -1, 0),
    (-1, 1, 0),
    (1, 0, 1),
    (-1, 0, -1),
    (1, 0, -1),
    (-1, 0, 1),
    (0, 1, 1),
    (0, -1, -1),
    (0, 1, -1),
    (0, -1, 1),
]
WEIGHTS = [1.0 / 3.0] + [1.0 / 18.0] * 6 + [1.0 / 36.0] * 12
OPPOSITE = [0, 2, 1, 4, 3, 6, 5, 8, 7, 10, 9, 12, 11, 14, 13, 16, 15, 18, 17]
WARMTH_LATTICE_W = [0.25] + [0.125] * 6
expansion_factor = 0.05


def padded_2(block, sides, width):
    for axis, dim in sides:
        count = lax.axis_size(axis)
        forward = [(i, i + 1) for i in range(count - 1)]
        backward = [(target, source) for source, target in forward]
        low = lax.ppermute(
            lax.slice_in_dim(block, block.shape[dim] - width, None, axis=dim), axis, forward
        )
        high = lax.ppermute(lax.slice_in_dim(block, 0, width, axis=dim), axis, backward)
        block = jnp.concatenate([low, block, high], axis=dim)
    return block


def relaxation_matrix():
    table = np.array(VELOCITY)
    px, py, pz = (table[:, 0], table[:, 1], table[:, 2])
    sq = px * px + py * py + pz * pz
    rows = [
        px * 0 + 1.0,
        19 * sq - 30.0,
        (21 * sq * sq - 53 * sq + 24) / 2.0,
        px * 1.0,
        (5 * sq - 9) * px * 1.0,
        py * 1.0,
        (5 * sq - 9) * py * 1.0,
        pz * 1.0,
        (5 * sq - 9) * pz * 1.0,
        3 * px * px - sq * 1.0,
        (3 * sq - 5) * (3 * px * px - sq) * 1.0,
        py * py - pz * pz * 1.0,
        (3 * sq - 5) * (py * py - pz * pz) * 1.0,
        px * py * 1.0,
        py * pz * 1.0,
        px * pz * 1.0,
        (py * py - pz * pz) * px * 1.0,
        (pz * pz - px * px) * py * 1.0,
        (px * px - py * py) * pz * 1.0,
    ]
    moment = np.stack(rows)
    inverse = moment.T / np.sum(moment * moment, axis=1)
    rates = np.array(
        [
            0.0,
            1.19,
            1.4,
            0.0,
            1.2,
            0.0,
            1.2,
            0.0,
            1.2,
            1.25,
            1.4,
            1.25,
            1.4,
            1.25,
            1.25,
            1.25,
            1.98,
            1.98,
            1.98,
        ]
    )
    return inverse * rates[None, :] @ moment


def flow_moments(flow_pops):
    density = jnp.sum(flow_pops, axis=0)
    momenta = []
    for axis_pick in range(3):
        total = jnp.zeros_like(density)
        for i in range(19):
            if VELOCITY[i][axis_pick] == 1:
                total = total + flow_pops[i]
            elif VELOCITY[i][axis_pick] == -1:
                total = total - flow_pops[i]
        momenta.append(total / density)
    return (density, momenta[0], momenta[1], momenta[2])


def equilibrium(i, density, vel_x, vel_y, vel_z, speed_sq):
    dir_x, dir_y, dir_z = VELOCITY[i]
    projected_speed = dir_x * vel_x + dir_y * vel_y + dir_z * vel_z
    return (
        WEIGHTS[i]
        * density
        * (1.0 + 3.0 * projected_speed + 4.5 * projected_speed * projected_speed - 1.5 * speed_sq)
    )


def collision(flow_pops, warmth_distribution, fill_mass, diffusivity, heat_source, cell_kind):
    density, vel_x, vel_y, vel_z = flow_moments(flow_pops)
    speed_sq = vel_x * vel_x + vel_y * vel_y + vel_z * vel_z
    cellwise_warmth = jnp.sum(warmth_distribution, axis=0)
    balance = jnp.stack([equilibrium(i, density, vel_x, vel_y, vel_z, speed_sq) for i in range(19)])
    kernel = jnp.asarray(relaxation_matrix(), dtype=jnp.float32)
    relaxed = jnp.einsum(
        "ij,jxyz->ixyz", kernel, flow_pops - balance, precision=lax.Precision.HIGHEST
    )
    lifting_push = expansion_factor * (cellwise_warmth - 1.0)
    post_flow = jnp.stack(
        [
            flow_pops[i] - relaxed[i] + 3.0 * WEIGHTS[i] * VELOCITY[i][2] * lifting_push
            for i in range(19)
        ]
    )
    relax_rate = 1.0 / (0.5 + 4.0 * diffusivity)
    post_list = []
    for warmth_lattice_vector in range(7):
        dir_x, dir_y, dir_z = VELOCITY[warmth_lattice_vector]
        projected_speed = dir_x * vel_x + dir_y * vel_y + dir_z * vel_z
        warmth_rest_state = (
            WARMTH_LATTICE_W[warmth_lattice_vector]
            * cellwise_warmth
            * (1.0 + 4.0 * projected_speed)
        )
        post_list.append(
            warmth_distribution[warmth_lattice_vector]
            - relax_rate * (warmth_distribution[warmth_lattice_vector] - warmth_rest_state)
            + WARMTH_LATTICE_W[warmth_lattice_vector] * heat_source
        )
    post_heat = jnp.stack(post_list)
    fill_frac = jnp.where(cell_kind == 1, fill_mass / density, jnp.where(cell_kind == 2, 1.0, 0.0))
    return (post_flow, post_heat, fill_frac)


def shift_depth(values, dir_z):
    if dir_z == 1:
        return jnp.concatenate([jnp.zeros_like(values[..., :1]), values[..., :-1]], axis=-1)
    if dir_z == -1:
        return jnp.concatenate([values[..., 1:], jnp.zeros_like(values[..., :1])], axis=-1)
    return values


def pull_from(padded, i, rows, cols):
    dir_x, dir_y, dir_z = VELOCITY[i]
    return shift_depth(padded[1 - dir_x : 1 - dir_x + rows, 1 - dir_y : 1 - dir_y + cols], dir_z)


def running(
    populations,
    frac_pad,
    kind_pad,
    flow_pops,
    warmth_distribution,
    fill_mass,
    fill_masks,
    cell_kind,
):
    rows, cols = (flow_pops.shape[1], flow_pops.shape[2])
    post_flow = populations[:19, 1:-1, 1:-1]
    post_heat = populations[19:, 1:-1, 1:-1]
    fill_frac = frac_pad[1:-1, 1:-1]
    density, vel_x, vel_y, vel_z = flow_moments(flow_pops)
    speed_sq = vel_x * vel_x + vel_y * vel_y + vel_z * vel_z
    unit_rho = jnp.ones_like(density)
    read = [post_flow[0]]
    mass_change = jnp.zeros_like(density)
    for i in range(1, 19):
        source_kind = pull_from(kind_pad, i, rows, cols)
        incoming = pull_from(populations[i], i, rows, cols)
        bounced = post_flow[OPPOSITE[i]]
        rebuilt = (
            equilibrium(i, unit_rho, vel_x, vel_y, vel_z, speed_sq)
            + equilibrium(OPPOSITE[i], unit_rho, vel_x, vel_y, vel_z, speed_sq)
            - bounced
        )
        read.append(
            jnp.where(source_kind == 3, bounced, jnp.where(source_kind == 0, rebuilt, incoming))
        )
        exchange_weight = jnp.where(
            source_kind == 2,
            1.0,
            jnp.where(
                source_kind == 1, 0.5 * (fill_frac + pull_from(frac_pad, i, rows, cols)), 0.0
            ),
        )
        mask_word = fill_masks[(i - 1) // 9]
        enabled = (mask_word // 2 ** ((i - 1) % 9) % 2).astype(density.dtype)
        mass_change = mass_change + enabled * exchange_weight * (incoming - bounced)
    heat_read = [post_heat[0]]
    for warmth_lattice_vector in range(1, 7):
        source_kind = pull_from(kind_pad, warmth_lattice_vector, rows, cols)
        incoming = pull_from(
            populations[19 + warmth_lattice_vector], warmth_lattice_vector, rows, cols
        )
        bounced = post_heat[OPPOSITE[warmth_lattice_vector]]
        heat_read.append(jnp.where((source_kind == 0) | (source_kind == 3), bounced, incoming))
    fluid = (cell_kind == 1) | (cell_kind == 2)
    flow_next = jnp.where(fluid[None], jnp.stack(read), flow_pops)
    heat_next = jnp.where(fluid[None], jnp.stack(heat_read), warmth_distribution)
    new_density = jnp.sum(flow_next, axis=0)
    mass_next = jnp.where(
        cell_kind == 1, fill_mass + mass_change, jnp.where(cell_kind == 2, new_density, 0.0)
    )
    return (flow_next, heat_next, mass_next)


def shards(
    flow_pops, warmth_distribution, fill_mass, diffusivity, heat_source, cell_kind, fill_masks
):
    kind_pad = padded_2(cell_kind, (("gx", 0), ("gy", 1)), 1)
    for iteration in range(ITERS):
        post_flow, post_heat, fill_frac = collision(
            flow_pops, warmth_distribution, fill_mass, diffusivity, heat_source, cell_kind
        )
        populations = jnp.concatenate([post_flow, post_heat], axis=0)
        padded, frac_wide = (
            padded_2(populations, (("gx", 1), ("gy", 2)), 1),
            padded_2(fill_frac[None], (("gx", 1), ("gy", 2)), 1),
        )
        frac_pad = frac_wide[0]
        flow_pops, warmth_distribution, fill_mass = running(
            padded,
            frac_pad,
            kind_pad,
            flow_pops,
            warmth_distribution,
            fill_mass,
            fill_masks,
            cell_kind,
        )
    return (flow_pops, warmth_distribution, fill_mass)


def solution(mesh):
    return jax.shard_map(
        shards,
        mesh=mesh,
        in_specs=(
            P(None, "gx", "gy", None),
            P(None, "gx", "gy", None),
            P("gx", "gy", None),
            P("gx", "gy", None),
            P("gx", "gy", None),
            P("gx", "gy", None),
            P(None, "gx", "gy", None),
        ),
        out_specs=(P(None, "gx", "gy", None), P(None, "gx", "gy", None), P("gx", "gy", None)),
        check_vma=False,
    )
```

profile of v0, /device:TPU:7, one launch (start us, length us, event | category | flops | bytes accessed | tf_op | source)
XLA Modules:
  0.0 152.5 jit_solution(14566580286380653955)
XLA Ops:
  1.4 12.0 %collective-permute-start.5 = (s32[1,8,128]{2,1,0:T(8,128)S(1)}, s32[1,8,128]{2,1,0:T(8,128)S(1)}, u32[]{:S(2)}, u32[]{:S(2)}) collective-permute-start(s32[1,8,128]{2,1,0:T(8,128)S(1)} %get-tuple-element.451), channel_id=1, source_target_pairs={{16,0},{32,16},{48,32},{64,48},{80,64},{96,80},{112,96},{128,112},... | collective-permute-start | bytes 12296 | tf_op jit(solution)/shard_map/ppermute | solution.py:45
  13.4 1.9 %collective-permute-start = (s32[1,8,128]{2,1,0:T(8,128)S(1)}, s32[1,8,128]{2,1,0:T(8,128)S(1)}, u32[]{:S(2)}, u32[]{:S(2)}) collective-permute-start(s32[1,8,128]{2,1,0:T(8,128)S(1)} %get-tuple-element.452), channel_id=1, source_target_pairs={{0,16},{16,32},{32,48},{48,64},{64,80},{80,96},{96,112},{112,128},... | collective-permute-start | bytes 12296 | tf_op jit(solution)/shard_map/ppermute | solution.py:42
  17.2 1.9 %collective-permute-start.16 = (f32[1,1,8,128]{3,2,1,0:T(8,128)S(1)}, f32[1,1,8,128]{3,2,1,0:T(8,128)S(1)}, u32[]{:S(2)}, u32[]{:S(2)}) collective-permute-start(f32[1,1,8,128]{3,2,1,0:T(8,128)S(1)} %get-tuple-element.444), channel_id=1, source_target_pairs={{0,16},{16,32},{32,48},{48,64},{64,80},{80,96},{96,112},{112,128},... | collective-permute-start | bytes 12296 | tf_op jit(solution)/shard_map/ppermute | solution.py:42
  19.1 7.0 %collective-permute-start.17 = (f32[1,1,8,128]{3,2,1,0:T(8,128)S(1)}, f32[1,1,8,128]{3,2,1,0:T(8,128)S(1)}, u32[]{:S(2)}, u32[]{:S(2)}) collective-permute-start(f32[1,1,8,128]{3,2,1,0:T(8,128)S(1)} %get-tuple-element.445), channel_id=1, source_target_pairs={{16,0},{32,16},{48,32},{64,48},{80,64},{96,80},{112,96},{128,112},... | collective-permute-start | bytes 12296 | tf_op jit(solution)/shard_map/ppermute | solution.py:45
  30.6 1.9 %collective-permute-start.1 = (f32[26,1,8,128]{3,2,1,0:T(8,128)S(1)}, f32[26,1,8,128]{3,2,1,0:T(8,128)S(1)}, u32[]{:S(2)}, u32[]{:S(2)}) collective-permute-start(f32[26,1,8,128]{3,2,1,0:T(8,128)S(1)} %get-tuple-element.328), channel_id=1, source_target_pairs={{0,16},{16,32},{32,48},{48,64},{64,80},{80,96},{96,112},{112,128},... | collective-permute-start | bytes 319496 | tf_op jit(solution)/shard_map/ppermute | solution.py:42
  32.7 7.0 %collective-permute-start.2 = (f32[26,1,8,128]{3,2,1,0:T(8,128)S(1)}, f32[26,1,8,128]{3,2,1,0:T(8,128)S(1)}, u32[]{:S(2)}, u32[]{:S(2)}) collective-permute-start(f32[26,1,8,128]{3,2,1,0:T(8,128)S(1)} %get-tuple-element.329), channel_id=1, source_target_pairs={{16,0},{32,16},{48,32},{64,48},{80,64},{96,80},{112,96},{128,112},... | collective-permute-start | bytes 319496 | tf_op jit(solution)/shard_map/ppermute | solution.py:45
  39.7 4.5 %collective-permute-start.18 = (f32[1,8,1,128]{3,2,1,0:T(1,128)S(1)}, f32[1,8,1,128]{3,2,1,0:T(1,128)S(1)}, u32[]{:S(2)}, u32[]{:S(2)}) collective-permute-start(f32[1,8,1,128]{3,2,1,0:T(1,128)S(1)} %get-tuple-element.430), channel_id=1, source_target_pairs={{0,1},{1,2},{2,3},{3,4},{4,5},{5,6},{6,7},{7,8},{8,9},{9,10},{10,1... | collective-permute-start | bytes 12296 | tf_op jit(solution)/shard_map/ppermute | solution.py:42
  44.2 1.9 %collective-permute-start.19 = (f32[1,8,1,128]{3,2,1,0:T(1,128)S(1)}, f32[1,8,1,128]{3,2,1,0:T(1,128)S(1)}, u32[]{:S(2)}, u32[]{:S(2)}) collective-permute-start(f32[1,8,1,128]{3,2,1,0:T(1,128)S(1)} %get-tuple-element.431), channel_id=1, source_target_pairs={{1,0},{2,1},{3,2},{4,3},{5,4},{6,5},{7,6},{8,7},{9,8},{10,9},{11,1... | collective-permute-start | bytes 12296 | tf_op jit(solution)/shard_map/ppermute | solution.py:45
  46.2 3.1 %collective-permute-start.7 = (s32[8,1,128]{2,1,0:T(1,128)S(1)}, s32[8,1,128]{2,1,0:T(1,128)S(1)}, u32[]{:S(2)}, u32[]{:S(2)}) collective-permute-start(s32[8,1,128]{2,1,0:T(1,128)S(1)} %get-tuple-element.434), channel_id=1, source_target_pairs={{1,0},{2,1},{3,2},{4,3},{5,4},{6,5},{7,6},{8,7},{9,8},{10,9},{11,1... | collective-permute-start | bytes 12296 | tf_op jit(solution)/shard_map/ppermute | solution.py:45
  49.5 3.4 %collective-permute-start.6 = (s32[8,1,128]{2,1,0:T(1,128)S(1)}, s32[8,1,128]{2,1,0:T(1,128)S(1)}, u32[]{:S(2)}, u32[]{:S(2)}) collective-permute-start(s32[8,1,128]{2,1,0:T(1,128)S(1)} %get-tuple-element.435), channel_id=1, source_target_pairs={{0,1},{1,2},{2,3},{3,4},{4,5},{5,6},{6,7},{7,8},{8,9},{9,10},{10,1... | collective-permute-start | bytes 12296 | tf_op jit(solution)/shard_map/ppermute | solution.py:42
  53.1 2.4 %collective-permute-start.3 = (f32[26,8,1,128]{3,2,1,0:T(1,128)S(1)}, f32[26,8,1,128]{3,2,1,0:T(1,128)S(1)}, u32[]{:S(2)}, u32[]{:S(2)}) collective-permute-start(f32[26,8,1,128]{3,2,1,0:T(1,128)S(1)} %get-tuple-element.322), channel_id=1, source_target_pairs={{0,1},{1,2},{2,3},{3,4},{4,5},{5,6},{6,7},{7,8},{8,9},{9,10},{10,1... | collective-permute-start | bytes 319496 | tf_op jit(solution)/shard_map/ppermute | solution.py:42
  55.5 1.9 %collective-permute-start.4 = (f32[26,8,1,128]{3,2,1,0:T(1,128)S(1)}, f32[26,8,1,128]{3,2,1,0:T(1,128)S(1)}, u32[]{:S(2)}, u32[]{:S(2)}) collective-permute-start(f32[26,8,1,128]{3,2,1,0:T(1,128)S(1)} %get-tuple-element.323), channel_id=1, source_target_pairs={{1,0},{2,1},{3,2},{4,3},{5,4},{6,5},{7,6},{8,7},{9,8},{10,9},{11,1... | collective-permute-start | bytes 319496 | tf_op jit(solution)/shard_map/ppermute | solution.py:45
  57.6 4.9 %collective-permute-done.4 = f32[26,8,1,128]{3,2,1,0:T(1,128)S(1)} collective-permute-done((f32[26,8,1,128]{3,2,1,0:T(1,128)S(1)}, f32[26,8,1,128]{3,2,1,0:T(1,128)S(1)}, u32[]{:S(2)}, u32[]{:S(2)}) %collective-permute-start.4) | collective-permute-done | bytes 106528 | tf_op jit(solution)/shard_map/ppermute | solution.py:45
  66.1 1.9 %collective-permute-start.20 = (f32[1,1,8,128]{3,2,1,0:T(8,128)S(1)}, f32[1,1,8,128]{3,2,1,0:T(8,128)S(1)}, u32[]{:S(2)}, u32[]{:S(2)}) collective-permute-start(f32[1,1,8,128]{3,2,1,0:T(8,128)S(1)} %get-tuple-element.442), channel_id=1, source_target_pairs={{0,16},{16,32},{32,48},{48,64},{64,80},{80,96},{96,112},{112,128},... | collective-permute-start | bytes 12296 | tf_op jit(solution)/shard_map/ppermute | solution.py:42
  68.0 7.0 %collective-permute-start.21 = (f32[1,1,8,128]{3,2,1,0:T(8,128)S(1)}, f32[1,1,8,128]{3,2,1,0:T(8,128)S(1)}, u32[]{:S(2)}, u32[]{:S(2)}) collective-permute-start(f32[1,1,8,128]{3,2,1,0:T(8,128)S(1)} %get-tuple-element.443), channel_id=1, source_target_pairs={{16,0},{32,16},{48,32},{64,48},{80,64},{96,80},{112,96},{128,112},... | collective-permute-start | bytes 12296 | tf_op jit(solution)/shard_map/ppermute | solution.py:45
  77.4 2.4 %collective-permute-start.22 = (f32[1,8,1,128]{3,2,1,0:T(1,128)S(1)}, f32[1,8,1,128]{3,2,1,0:T(1,128)S(1)}, u32[]{:S(2)}, u32[]{:S(2)}) collective-permute-start(f32[1,8,1,128]{3,2,1,0:T(1,128)S(1)} %get-tuple-element.428), channel_id=1, source_target_pairs={{0,1},{1,2},{2,3},{3,4},{4,5},{5,6},{6,7},{7,8},{8,9},{9,10},{10,1... | collective-permute-start | bytes 12296 | tf_op jit(solution)/shard_map/ppermute | solution.py:42
  79.8 2.0 %collective-permute-start.23 = (f32[1,8,1,128]{3,2,1,0:T(1,128)S(1)}, f32[1,8,1,128]{3,2,1,0:T(1,128)S(1)}, u32[]{:S(2)}, u32[]{:S(2)}) collective-permute-start(f32[1,8,1,128]{3,2,1,0:T(1,128)S(1)} %get-tuple-element.429), channel_id=1, source_target_pairs={{1,0},{2,1},{3,2},{4,3},{5,4},{6,5},{7,6},{8,7},{9,8},{10,9},{11,1... | collective-permute-start | bytes 12296 | tf_op jit(solution)/shard_map/ppermute | solution.py:45
  81.8 1.9 %collective-permute-start.8 = (f32[26,1,8,128]{3,2,1,0:T(8,128)S(1)}, f32[26,1,8,128]{3,2,1,0:T(8,128)S(1)}, u32[]{:S(2)}, u32[]{:S(2)}) collective-permute-start(f32[26,1,8,128]{3,2,1,0:T(8,128)S(1)} %get-tuple-element.326), channel_id=1, source_target_pairs={{0,16},{16,32},{32,48},{48,64},{64,80},{80,96},{96,112},{112,128},... | collective-permute-start | bytes 319496 | tf_op jit(solution)/shard_map/ppermute | solution.py:42
  83.7 7.0 %collective-permute-start.9 = (f32[26,1,8,128]{3,2,1,0:T(8,128)S(1)}, f32[26,1,8,128]{3,2,1,0:T(8,128)S(1)}, u32[]{:S(2)}, u32[]{:S(2)}) collective-permute-start(f32[26,1,8,128]{3,2,1,0:T(8,128)S(1)} %get-tuple-element.327), channel_id=1, source_target_pairs={{16,0},{32,16},{48,32},{64,48},{80,64},{96,80},{112,96},{128,112},... | collective-permute-start | bytes 319496 | tf_op jit(solution)/shard_map/ppermute | solution.py:45
  92.9 5.2 %collective-permute-start.10 = (f32[26,8,1,128]{3,2,1,0:T(1,128)S(1)}, f32[26,8,1,128]{3,2,1,0:T(1,128)S(1)}, u32[]{:S(2)}, u32[]{:S(2)}) collective-permute-start(f32[26,8,1,128]{3,2,1,0:T(1,128)S(1)} %get-tuple-element.320), channel_id=1, source_target_pairs={{0,1},{1,2},{2,3},{3,4},{4,5},{5,6},{6,7},{7,8},{8,9},{9,10},{10,1... | collective-permute-start | bytes 319496 | tf_op jit(solution)/shard_map/ppermute | solution.py:42
  98.2 1.9 %collective-permute-start.11 = (f32[26,8,1,128]{3,2,1,0:T(1,128)S(1)}, f32[26,8,1,128]{3,2,1,0:T(1,128)S(1)}, u32[]{:S(2)}, u32[]{:S(2)}) collective-permute-start(f32[26,8,1,128]{3,2,1,0:T(1,128)S(1)} %get-tuple-element.321), channel_id=1, source_target_pairs={{1,0},{2,1},{3,2},{4,3},{5,4},{6,5},{7,6},{8,7},{9,8},{10,9},{11,1... | collective-permute-start | bytes 319496 | tf_op jit(solution)/shard_map/ppermute | solution.py:45
  100.2 4.9 %collective-permute-done.11 = f32[26,8,1,128]{3,2,1,0:T(1,128)S(1)} collective-permute-done((f32[26,8,1,128]{3,2,1,0:T(1,128)S(1)}, f32[26,8,1,128]{3,2,1,0:T(1,128)S(1)}, u32[]{:S(2)}, u32[]{:S(2)}) %collective-permute-start.11) | collective-permute-done | bytes 106528 | tf_op jit(solution)/shard_map/ppermute | solution.py:45
  107.8 1.9 %collective-permute-start.24 = (f32[1,1,8,128]{3,2,1,0:T(8,128)S(1)}, f32[1,1,8,128]{3,2,1,0:T(8,128)S(1)}, u32[]{:S(2)}, u32[]{:S(2)}) collective-permute-start(f32[1,1,8,128]{3,2,1,0:T(8,128)S(1)} %get-tuple-element.440), channel_id=1, source_target_pairs={{0,16},{16,32},{32,48},{48,64},{64,80},{80,96},{96,112},{112,128},... | collective-permute-start | bytes 12296 | tf_op jit(solution)/shard_map/ppermute | solution.py:42
  109.7 8.4 %collective-permute-start.25 = (f32[1,1,8,128]{3,2,1,0:T(8,128)S(1)}, f32[1,1,8,128]{3,2,1,0:T(8,128)S(1)}, u32[]{:S(2)}, u32[]{:S(2)}) collective-permute-start(f32[1,1,8,128]{3,2,1,0:T(8,128)S(1)} %get-tuple-element.441), channel_id=1, source_target_pairs={{16,0},{32,16},{48,32},{64,48},{80,64},{96,80},{112,96},{128,112},... | collective-permute-start | bytes 12296 | tf_op jit(solution)/shard_map/ppermute | solution.py:45
  120.6 1.9 %collective-permute-start.26 = (f32[1,8,1,128]{3,2,1,0:T(1,128)S(1)}, f32[1,8,1,128]{3,2,1,0:T(1,128)S(1)}, u32[]{:S(2)}, u32[]{:S(2)}) collective-permute-start(f32[1,8,1,128]{3,2,1,0:T(1,128)S(1)} %get-tuple-element.426), channel_id=1, source_target_pairs={{0,1},{1,2},{2,3},{3,4},{4,5},{5,6},{6,7},{7,8},{8,9},{9,10},{10,1... | collective-permute-start | bytes 12296 | tf_op jit(solution)/shard_map/ppermute | solution.py:42
  122.5 2.4 %collective-permute-start.27 = (f32[1,8,1,128]{3,2,1,0:T(1,128)S(1)}, f32[1,8,1,128]{3,2,1,0:T(1,128)S(1)}, u32[]{:S(2)}, u32[]{:S(2)}) collective-permute-start(f32[1,8,1,128]{3,2,1,0:T(1,128)S(1)} %get-tuple-element.427), channel_id=1, source_target_pairs={{1,0},{2,1},{3,2},{4,3},{5,4},{6,5},{7,6},{8,7},{9,8},{10,9},{11,1... | collective-permute-start | bytes 12296 | tf_op jit(solution)/shard_map/ppermute | solution.py:45
  125.0 1.9 %collective-permute-start.12 = (f32[26,1,8,128]{3,2,1,0:T(8,128)S(1)}, f32[26,1,8,128]{3,2,1,0:T(8,128)S(1)}, u32[]{:S(2)}, u32[]{:S(2)}) collective-permute-start(f32[26,1,8,128]{3,2,1,0:T(8,128)S(1)} %get-tuple-element.324), channel_id=1, source_target_pairs={{0,16},{16,32},{32,48},{48,64},{64,80},{80,96},{96,112},{112,128},... | collective-permute-start | bytes 319496 | tf_op jit(solution)/shard_map/ppermute | solution.py:42
  126.9 7.0 %collective-permute-start.13 = (f32[26,1,8,128]{3,2,1,0:T(8,128)S(1)}, f32[26,1,8,128]{3,2,1,0:T(8,128)S(1)}, u32[]{:S(2)}, u32[]{:S(2)}) collective-permute-start(f32[26,1,8,128]{3,2,1,0:T(8,128)S(1)} %get-tuple-element.325), channel_id=1, source_target_pairs={{16,0},{32,16},{48,32},{64,48},{80,64},{96,80},{112,96},{128,112},... | collective-permute-start | bytes 319496 | tf_op jit(solution)/shard_map/ppermute | solution.py:45
  136.0 4.8 %collective-permute-start.14 = (f32[26,8,1,128]{3,2,1,0:T(1,128)S(1)}, f32[26,8,1,128]{3,2,1,0:T(1,128)S(1)}, u32[]{:S(2)}, u32[]{:S(2)}) collective-permute-start(f32[26,8,1,128]{3,2,1,0:T(1,128)S(1)} %get-tuple-element.318), channel_id=1, source_target_pairs={{0,1},{1,2},{2,3},{3,4},{4,5},{5,6},{6,7},{7,8},{8,9},{9,10},{10,1... | collective-permute-start | bytes 319496 | tf_op jit(solution)/shard_map/ppermute | solution.py:42
  140.9 1.9 %collective-permute-start.15 = (f32[26,8,1,128]{3,2,1,0:T(1,128)S(1)}, f32[26,8,1,128]{3,2,1,0:T(1,128)S(1)}, u32[]{:S(2)}, u32[]{:S(2)}) collective-permute-start(f32[26,8,1,128]{3,2,1,0:T(1,128)S(1)} %get-tuple-element.319), channel_id=1, source_target_pairs={{1,0},{2,1},{3,2},{4,3},{5,4},{6,5},{7,6},{8,7},{9,8},{10,9},{11,1... | collective-permute-start | bytes 319496 | tf_op jit(solution)/shard_map/ppermute | solution.py:45
  142.9 4.9 %collective-permute-done.15 = f32[26,8,1,128]{3,2,1,0:T(1,128)S(1)} collective-permute-done((f32[26,8,1,128]{3,2,1,0:T(1,128)S(1)}, f32[26,8,1,128]{3,2,1,0:T(1,128)S(1)}, u32[]{:S(2)}, u32[]{:S(2)}) %collective-permute-start.15) | collective-permute-done | bytes 106528 | tf_op jit(solution)/shard_map/ppermute | solution.py:45
  151.2 1.2 fusion.416
  (361 shorter events, 25.3 us)
Async XLA Ops:
  0.6 25.5 %copy-start = (f32[19,6,8,128]{3,2,1,0:T(8,128)S(1)}, f32[19,6,8,128]{3,2,1,0:T(8,128)}, u32[]{:S(2)}) copy-start(f32[19,6,8,128]{3,2,1,0:T(8,128)} %param.10) | copy-start | bytes 1400836
  1.4 44.8 %collective-permute-start.5 = (s32[1,8,128]{2,1,0:T(8,128)S(1)}, s32[1,8,128]{2,1,0:T(8,128)S(1)}, u32[]{:S(2)}, u32[]{:S(2)}) collective-permute-start(s32[1,8,128]{2,1,0:T(8,128)S(1)} %get-tuple-element.451), channel_id=1, source_target_pairs={{16,0},{32,16},{48,32},{64,48},{80,64},{96,80},{112,96},{128,112},... | collective-permute-start | bytes 12296 | tf_op jit(solution)/shard_map/ppermute | solution.py:45
  13.4 3.0 %copy-start.4 = (s32[6,8,128]{2,1,0:T(8,128)S(1)}, s32[6,8,128]{2,1,0:T(8,128)}, u32[]{:S(2)}) copy-start(s32[6,8,128]{2,1,0:T(8,128)} %param.15) | copy-start | bytes 73732
  13.4 30.8 %collective-permute-start = (s32[1,8,128]{2,1,0:T(8,128)S(1)}, s32[1,8,128]{2,1,0:T(8,128)S(1)}, u32[]{:S(2)}, u32[]{:S(2)}) collective-permute-start(s32[1,8,128]{2,1,0:T(8,128)S(1)} %get-tuple-element.452), channel_id=1, source_target_pairs={{0,16},{16,32},{32,48},{48,64},{64,80},{80,96},{96,112},{112,128},... | collective-permute-start | bytes 12296 | tf_op jit(solution)/shard_map/ppermute | solution.py:42
  16.4 9.7 %copy-start.3 = (f32[7,6,8,128]{3,2,1,0:T(8,128)S(1)}, f32[7,6,8,128]{3,2,1,0:T(8,128)}, u32[]{:S(2)}) copy-start(f32[7,6,8,128]{3,2,1,0:T(8,128)} %param.11) | copy-start | bytes 516100
  17.2 15.5 %collective-permute-start.16 = (f32[1,1,8,128]{3,2,1,0:T(8,128)S(1)}, f32[1,1,8,128]{3,2,1,0:T(8,128)S(1)}, u32[]{:S(2)}, u32[]{:S(2)}) collective-permute-start(f32[1,1,8,128]{3,2,1,0:T(8,128)S(1)} %get-tuple-element.444), channel_id=1, source_target_pairs={{0,16},{16,32},{32,48},{48,64},{64,80},{80,96},{96,112},{112,128},... | collective-permute-start | bytes 12296 | tf_op jit(solution)/shard_map/ppermute | solution.py:42
  19.1 20.5 %collective-permute-start.17 = (f32[1,1,8,128]{3,2,1,0:T(8,128)S(1)}, f32[1,1,8,128]{3,2,1,0:T(8,128)S(1)}, u32[]{:S(2)}, u32[]{:S(2)}) collective-permute-start(f32[1,1,8,128]{3,2,1,0:T(8,128)S(1)} %get-tuple-element.445), channel_id=1, source_target_pairs={{16,0},{32,16},{48,32},{64,48},{80,64},{96,80},{112,96},{128,112},... | collective-permute-start | bytes 12296 | tf_op jit(solution)/shard_map/ppermute | solution.py:45
  30.6 22.3 %collective-permute-start.1 = (f32[26,1,8,128]{3,2,1,0:T(8,128)S(1)}, f32[26,1,8,128]{3,2,1,0:T(8,128)S(1)}, u32[]{:S(2)}, u32[]{:S(2)}) collective-permute-start(f32[26,1,8,128]{3,2,1,0:T(8,128)S(1)} %get-tuple-element.328), channel_id=1, source_target_pairs={{0,16},{16,32},{32,48},{48,64},{64,80},{80,96},{96,112},{112,128},... | collective-permute-start | bytes 319496 | tf_op jit(solution)/shard_map/ppermute | solution.py:42
  32.7 20.3 %collective-permute-start.2 = (f32[26,1,8,128]{3,2,1,0:T(8,128)S(1)}, f32[26,1,8,128]{3,2,1,0:T(8,128)S(1)}, u32[]{:S(2)}, u32[]{:S(2)}) collective-permute-start(f32[26,1,8,128]{3,2,1,0:T(8,128)S(1)} %get-tuple-element.329), channel_id=1, source_target_pairs={{16,0},{32,16},{48,32},{64,48},{80,64},{96,80},{112,96},{128,112},... | collective-permute-start | bytes 319496 | tf_op jit(solution)/shard_map/ppermute | solution.py:45
  39.7 9.8 %collective-permute-start.18 = (f32[1,8,1,128]{3,2,1,0:T(1,128)S(1)}, f32[1,8,1,128]{3,2,1,0:T(1,128)S(1)}, u32[]{:S(2)}, u32[]{:S(2)}) collective-permute-start(f32[1,8,1,128]{3,2,1,0:T(1,128)S(1)} %get-tuple-element.430), channel_id=1, source_target_pairs={{0,1},{1,2},{2,3},{3,4},{4,5},{5,6},{6,7},{7,8},{8,9},{9,10},{10,1... | collective-permute-start | bytes 12296 | tf_op jit(solution)/shard_map/ppermute | solution.py:42
  44.2 8.6 %collective-permute-start.19 = (f32[1,8,1,128]{3,2,1,0:T(1,128)S(1)}, f32[1,8,1,128]{3,2,1,0:T(1,128)S(1)}, u32[]{:S(2)}, u32[]{:S(2)}) collective-permute-start(f32[1,8,1,128]{3,2,1,0:T(1,128)S(1)} %get-tuple-element.431), channel_id=1, source_target_pairs={{1,0},{2,1},{3,2},{4,3},{5,4},{6,5},{7,6},{8,7},{9,8},{10,9},{11,1... | collective-permute-start | bytes 12296 | tf_op jit(solution)/shard_map/ppermute | solution.py:45
  46.2 11.3 %collective-permute-start.7 = (s32[8,1,128]{2,1,0:T(1,128)S(1)}, s32[8,1,128]{2,1,0:T(1,128)S(1)}, u32[]{:S(2)}, u32[]{:S(2)}) collective-permute-start(s32[8,1,128]{2,1,0:T(1,128)S(1)} %get-tuple-element.434), channel_id=1, source_target_pairs={{1,0},{2,1},{3,2},{4,3},{5,4},{6,5},{7,6},{8,7},{9,8},{10,9},{11,1... | collective-permute-start | bytes 12296 | tf_op jit(solution)/shard_map/ppermute | solution.py:45
  49.5 8.0 %collective-permute-start.6 = (s32[8,1,128]{2,1,0:T(1,128)S(1)}, s32[8,1,128]{2,1,0:T(1,128)S(1)}, u32[]{:S(2)}, u32[]{:S(2)}) collective-permute-start(s32[8,1,128]{2,1,0:T(1,128)S(1)} %get-tuple-element.435), channel_id=1, source_target_pairs={{0,1},{1,2},{2,3},{3,4},{4,5},{5,6},{6,7},{7,8},{8,9},{9,10},{10,1... | collective-permute-start | bytes 12296 | tf_op jit(solution)/shard_map/ppermute | solution.py:42
  53.1 4.5 %collective-permute-start.3 = (f32[26,8,1,128]{3,2,1,0:T(1,128)S(1)}, f32[26,8,1,128]{3,2,1,0:T(1,128)S(1)}, u32[]{:S(2)}, u32[]{:S(2)}) collective-permute-start(f32[26,8,1,128]{3,2,1,0:T(1,128)S(1)} %get-tuple-element.322), channel_id=1, source_target_pairs={{0,1},{1,2},{2,3},{3,4},{4,5},{5,6},{6,7},{7,8},{8,9},{9,10},{10,1... | collective-permute-start | bytes 319496 | tf_op jit(solution)/shard_map/ppermute | solution.py:42
  55.5 6.9 %collective-permute-start.4 = (f32[26,8,1,128]{3,2,1,0:T(1,128)S(1)}, f32[26,8,1,128]{3,2,1,0:T(1,128)S(1)}, u32[]{:S(2)}, u32[]{:S(2)}) collective-permute-start(f32[26,8,1,128]{3,2,1,0:T(1,128)S(1)} %get-tuple-element.323), channel_id=1, source_target_pairs={{1,0},{2,1},{3,2},{4,3},{5,4},{6,5},{7,6},{8,7},{9,8},{10,9},{11,1... | collective-permute-start | bytes 319496 | tf_op jit(solution)/shard_map/ppermute | solution.py:45
  64.5 0.8 copy-start.5
  66.1 11.3 %collective-permute-start.20 = (f32[1,1,8,128]{3,2,1,0:T(8,128)S(1)}, f32[1,1,8,128]{3,2,1,0:T(8,128)S(1)}, u32[]{:S(2)}, u32[]{:S(2)}) collective-permute-start(f32[1,1,8,128]{3,2,1,0:T(8,128)S(1)} %get-tuple-element.442), channel_id=1, source_target_pairs={{0,16},{16,32},{32,48},{48,64},{64,80},{80,96},{96,112},{112,128},... | collective-permute-start | bytes 12296 | tf_op jit(solution)/shard_map/ppermute | solution.py:42
  68.0 9.4 %collective-permute-start.21 = (f32[1,1,8,128]{3,2,1,0:T(8,128)S(1)}, f32[1,1,8,128]{3,2,1,0:T(8,128)S(1)}, u32[]{:S(2)}, u32[]{:S(2)}) collective-permute-start(f32[1,1,8,128]{3,2,1,0:T(8,128)S(1)} %get-tuple-element.443), channel_id=1, source_target_pairs={{16,0},{32,16},{48,32},{64,48},{80,64},{96,80},{112,96},{128,112},... | collective-permute-start | bytes 12296 | tf_op jit(solution)/shard_map/ppermute | solution.py:45
  77.4 13.3 %collective-permute-start.22 = (f32[1,8,1,128]{3,2,1,0:T(1,128)S(1)}, f32[1,8,1,128]{3,2,1,0:T(1,128)S(1)}, u32[]{:S(2)}, u32[]{:S(2)}) collective-permute-start(f32[1,8,1,128]{3,2,1,0:T(1,128)S(1)} %get-tuple-element.428), channel_id=1, source_target_pairs={{0,1},{1,2},{2,3},{3,4},{4,5},{5,6},{6,7},{7,8},{8,9},{9,10},{10,1... | collective-permute-start | bytes 12296 | tf_op jit(solution)/shard_map/ppermute | solution.py:42
  79.8 10.9 %collective-permute-start.23 = (f32[1,8,1,128]{3,2,1,0:T(1,128)S(1)}, f32[1,8,1,128]{3,2,1,0:T(1,128)S(1)}, u32[]{:S(2)}, u32[]{:S(2)}) collective-permute-start(f32[1,8,1,128]{3,2,1,0:T(1,128)S(1)} %get-tuple-element.429), channel_id=1, source_target_pairs={{1,0},{2,1},{3,2},{4,3},{5,4},{6,5},{7,6},{8,7},{9,8},{10,9},{11,1... | collective-permute-start | bytes 12296 | tf_op jit(solution)/shard_map/ppermute | solution.py:45
  81.8 10.1 %collective-permute-start.8 = (f32[26,1,8,128]{3,2,1,0:T(8,128)S(1)}, f32[26,1,8,128]{3,2,1,0:T(8,128)S(1)}, u32[]{:S(2)}, u32[]{:S(2)}) collective-permute-start(f32[26,1,8,128]{3,2,1,0:T(8,128)S(1)} %get-tuple-element.326), channel_id=1, source_target_pairs={{0,16},{16,32},{32,48},{48,64},{64,80},{80,96},{96,112},{112,128},... | collective-permute-start | bytes 319496 | tf_op jit(solution)/shard_map/ppermute | solution.py:42
  83.7 9.1 %collective-permute-start.9 = (f32[26,1,8,128]{3,2,1,0:T(8,128)S(1)}, f32[26,1,8,128]{3,2,1,0:T(8,128)S(1)}, u32[]{:S(2)}, u32[]{:S(2)}) collective-permute-start(f32[26,1,8,128]{3,2,1,0:T(8,128)S(1)} %get-tuple-element.327), channel_id=1, source_target_pairs={{16,0},{32,16},{48,32},{64,48},{80,64},{96,80},{112,96},{128,112},... | collective-permute-start | bytes 319496 | tf_op jit(solution)/shard_map/ppermute | solution.py:45
  92.9 7.3 %collective-permute-start.10 = (f32[26,8,1,128]{3,2,1,0:T(1,128)S(1)}, f32[26,8,1,128]{3,2,1,0:T(1,128)S(1)}, u32[]{:S(2)}, u32[]{:S(2)}) collective-permute-start(f32[26,8,1,128]{3,2,1,0:T(1,128)S(1)} %get-tuple-element.320), channel_id=1, source_target_pairs={{0,1},{1,2},{2,3},{3,4},{4,5},{5,6},{6,7},{7,8},{8,9},{9,10},{10,1... | collective-permute-start | bytes 319496 | tf_op jit(solution)/shard_map/ppermute | solution.py:42
  98.2 6.9 %collective-permute-start.11 = (f32[26,8,1,128]{3,2,1,0:T(1,128)S(1)}, f32[26,8,1,128]{3,2,1,0:T(1,128)S(1)}, u32[]{:S(2)}, u32[]{:S(2)}) collective-permute-start(f32[26,8,1,128]{3,2,1,0:T(1,128)S(1)} %get-tuple-element.321), channel_id=1, source_target_pairs={{1,0},{2,1},{3,2},{4,3},{5,4},{6,5},{7,6},{8,7},{9,8},{10,9},{11,1... | collective-permute-start | bytes 319496 | tf_op jit(solution)/shard_map/ppermute | solution.py:45
  107.8 12.7 %collective-permute-start.24 = (f32[1,1,8,128]{3,2,1,0:T(8,128)S(1)}, f32[1,1,8,128]{3,2,1,0:T(8,128)S(1)}, u32[]{:S(2)}, u32[]{:S(2)}) collective-permute-start(f32[1,1,8,128]{3,2,1,0:T(8,128)S(1)} %get-tuple-element.440), channel_id=1, source_target_pairs={{0,16},{16,32},{32,48},{48,64},{64,80},{80,96},{96,112},{112,128},... | collective-permute-start | bytes 12296 | tf_op jit(solution)/shard_map/ppermute | solution.py:42
  109.7 10.8 %collective-permute-start.25 = (f32[1,1,8,128]{3,2,1,0:T(8,128)S(1)}, f32[1,1,8,128]{3,2,1,0:T(8,128)S(1)}, u32[]{:S(2)}, u32[]{:S(2)}) collective-permute-start(f32[1,1,8,128]{3,2,1,0:T(8,128)S(1)} %get-tuple-element.441), channel_id=1, source_target_pairs={{16,0},{32,16},{48,32},{64,48},{80,64},{96,80},{112,96},{128,112},... | collective-permute-start | bytes 12296 | tf_op jit(solution)/shard_map/ppermute | solution.py:45
  120.6 13.3 %collective-permute-start.26 = (f32[1,8,1,128]{3,2,1,0:T(1,128)S(1)}, f32[1,8,1,128]{3,2,1,0:T(1,128)S(1)}, u32[]{:S(2)}, u32[]{:S(2)}) collective-permute-start(f32[1,8,1,128]{3,2,1,0:T(1,128)S(1)} %get-tuple-element.426), channel_id=1, source_target_pairs={{0,1},{1,2},{2,3},{3,4},{4,5},{5,6},{6,7},{7,8},{8,9},{9,10},{10,1... | collective-permute-start | bytes 12296 | tf_op jit(solution)/shard_map/ppermute | solution.py:42
  122.5 11.4 %collective-permute-start.27 = (f32[1,8,1,128]{3,2,1,0:T(1,128)S(1)}, f32[1,8,1,128]{3,2,1,0:T(1,128)S(1)}, u32[]{:S(2)}, u32[]{:S(2)}) collective-permute-start(f32[1,8,1,128]{3,2,1,0:T(1,128)S(1)} %get-tuple-element.427), channel_id=1, source_target_pairs={{1,0},{2,1},{3,2},{4,3},{5,4},{6,5},{7,6},{8,7},{9,8},{10,9},{11,1... | collective-permute-start | bytes 12296 | tf_op jit(solution)/shard_map/ppermute | solution.py:45
  125.0 10.1 %collective-permute-start.12 = (f32[26,1,8,128]{3,2,1,0:T(8,128)S(1)}, f32[26,1,8,128]{3,2,1,0:T(8,128)S(1)}, u32[]{:S(2)}, u32[]{:S(2)}) collective-permute-start(f32[26,1,8,128]{3,2,1,0:T(8,128)S(1)} %get-tuple-element.324), channel_id=1, source_target_pairs={{0,16},{16,32},{32,48},{48,64},{64,80},{80,96},{96,112},{112,128},... | collective-permute-start | bytes 319496 | tf_op jit(solution)/shard_map/ppermute | solution.py:42
  126.9 9.0 %collective-permute-start.13 = (f32[26,1,8,128]{3,2,1,0:T(8,128)S(1)}, f32[26,1,8,128]{3,2,1,0:T(8,128)S(1)}, u32[]{:S(2)}, u32[]{:S(2)}) collective-permute-start(f32[26,1,8,128]{3,2,1,0:T(8,128)S(1)} %get-tuple-element.325), channel_id=1, source_target_pairs={{16,0},{32,16},{48,32},{64,48},{80,64},{96,80},{112,96},{128,112},... | collective-permute-start | bytes 319496 | tf_op jit(solution)/shard_map/ppermute | solution.py:45
  136.0 6.9 %collective-permute-start.14 = (f32[26,8,1,128]{3,2,1,0:T(1,128)S(1)}, f32[26,8,1,128]{3,2,1,0:T(1,128)S(1)}, u32[]{:S(2)}, u32[]{:S(2)}) collective-permute-start(f32[26,8,1,128]{3,2,1,0:T(1,128)S(1)} %get-tuple-element.318), channel_id=1, source_target_pairs={{0,1},{1,2},{2,3},{3,4},{4,5},{5,6},{6,7},{7,8},{8,9},{9,10},{10,1... | collective-permute-start | bytes 319496 | tf_op jit(solution)/shard_map/ppermute | solution.py:42
  140.9 6.9 %collective-permute-start.15 = (f32[26,8,1,128]{3,2,1,0:T(1,128)S(1)}, f32[26,8,1,128]{3,2,1,0:T(1,128)S(1)}, u32[]{:S(2)}, u32[]{:S(2)}) collective-permute-start(f32[26,8,1,128]{3,2,1,0:T(1,128)S(1)} %get-tuple-element.319), channel_id=1, source_target_pairs={{1,0},{2,1},{3,2},{4,3},{5,4},{6,5},{7,6},{8,7},{9,8},{10,9},{11,1... | collective-permute-start | bytes 319496 | tf_op jit(solution)/shard_map/ppermute | solution.py:45
  (5 other events, 3.7 us)
where the time goes:
time: 154 us; the launch traced here: 152 us
  starting transfers between devices  109 us (71%)
  waiting for transfers between devices  18.7 us (12%)
  other arithmetic  14.1 us (9%)
  local copies, waits for them, and re-layouts  6.25 us (4%)
  between operations  2.74 us (2%)
  matrix products  2.12 us (1%)
    ppermute x14, starting transfers between devices, padded_2(): lax.ppermute(lax.slice_in_dim(block, 0, width, axis=dim), axis, backward)  70.4 us
    ppermute x14, starting transfers between devices, padded_2(): lax.ppermute(lax.slice_in_dim(block, block.shape[dim] - width, None, axis...  38.1 us
    ppermute x14, waiting for transfers between devices, padded_2(): lax.ppermute(lax.slice_in_dim(block, 0, width, axis=dim), axis, backward)  16.4 us
    unnamed x194, other arithmetic  5.41 us
  transfers between devices with their start and end apart: 28, of which 7 were waited for; matrix products, arithmetic and copies ran while one was open for 6% of the time, Pallas kernels for 0%

commit v1 on v0

v1 whole, which is shorter than its diff:
```python
import functools

import jax
import jax.numpy as jnp
from jax import lax
from jax.experimental import pallas as pl
from jax.experimental.pallas import tpu as pltpu
from jax.sharding import PartitionSpec as P

ITERS = 3
VELOCITY = [
    (0, 0, 0),
    (1, 0, 0),
    (-1, 0, 0),
    (0, 1, 0),
    (0, -1, 0),
    (0, 0, 1),
    (0, 0, -1),
    (1, 1, 0),
    (-1, -1, 0),
    (1, -1, 0),
    (-1, 1, 0),
    (1, 0, 1),
    (-1, 0, -1),
    (1, 0, -1),
    (-1, 0, 1),
    (0, 1, 1),
    (0, -1, -1),
    (0, 1, -1),
    (0, -1, 1),
]
WEIGHTS = [1.0 / 3.0] + [1.0 / 18.0] * 6 + [1.0 / 36.0] * 12
OPPOSITE = [0, 2, 1, 4, 3, 6, 5, 8, 7, 10, 9, 12, 11, 14, 13, 16, 15, 18, 17]
EXPANSION = 0.05
MESH = pl.DeviceIdType.MESH
ROWS, SUB, LANE = 6, 8, 128

FRAC, KIND_A, KIND_B = 26, 27, 28
X_FIELDS = [
    [KIND_A, 1, 7, 9, 11, 13, 20, FRAC, 2, 8, 10, 12, 14, 21, KIND_B],
    [1, 7, 9, 11, 13, 20, FRAC, 2, 8, 10, 12, 14, 21],
]
Y_FIELDS = [
    {1: [3, 15, 17, 22, KIND_A, 7, FRAC, 10, KIND_B], -1: [4, 16, 18, 23, KIND_A, 9, FRAC, 8, KIND_B]},
    {1: [3, 15, 17, 22, 7, FRAC, 10], -1: [4, 16, 18, 23, 9, FRAC, 8]},
]
CLASSES = [(1, 0), (-1, 0), (1, 1), (1, -1), (-1, 1), (-1, -1), (0, 1), (0, -1)]


def x_index(rd, field):
    return X_FIELDS[min(rd, 1)].index(field)


def y_index(rd, dy, field):
    return Y_FIELDS[min(rd, 1)][dy].index(field)


def roll_y(value, dy):
    return pltpu.roll(value, dy % SUB, 0) if dy else value


def roll_z(value, dz):
    return pltpu.roll(value, dz % LANE, 1) if dz else value


def collide(f, g, mass, rate, heat, kind):
    (sa, sb, sc, sd, se, sf, sg, sh, si) = [f[i] + f[i + 1] for i in range(1, 19, 2)]
    (da, db, dc, dd, de, df, dg, dh, di) = [f[i] - f[i + 1] for i in range(1, 19, 2)]
    sxy, sxz, syz = sd + se, sf + sg, sh + si
    sbc = sb + sc
    sax = sa + sbc
    sdg = sxy + sxz + syz
    rho = f[0] + sax + sdg
    xde, xfg = dd + de, df + dg
    yde, yhi = dd - de, dh + di
    zfg, zhi = df - dg, dh - di
    xs, ys, zs = xde + xfg, yde + yhi, zfg + zhi
    jx, jy, jz = da + xs, db + ys, dc + zs
    inv = 1.0 / rho
    ux, uy, uz = jx * inv, jy * inv, jz * inv
    xx, yy, zz = jx * ux, jy * uy, jz * uz
    ruu = xx + yy + zz
    ae = (1.19 * 19.0 / 2394.0) * (sdg - f[0] - ruu)
    ap = (1.4 / 252.0) * (9.0 * f[0] - 7.0 * sax - 2.0 * sdg + 5.5 * ruu)
    qxx, qww = 2.0 * xx - yy - zz, yy - zz
    t1, t2 = 2.0 * sa - sbc, sxy + sxz - 2.0 * syz
    w1, w2 = sb - sc, sxy - sxz
    b = (1.25 / 36.0) * (t1 + t2 - qxx)
    bp = (1.4 / 72.0) * (t2 - 2.0 * t1 + 0.5 * qxx)
    c = (1.25 / 12.0) * (w1 + w2 - qww)
    cp = (1.4 / 24.0) * (w2 - 2.0 * w1 + 0.5 * qww)
    dxy = (1.25 / 4.0) * (sd - se - jx * uy)
    dyz = (1.25 / 4.0) * (sh - si - jy * uz)
    dxz = (1.25 / 4.0) * (sf - sg - jx * uz)
    q = 1.2 / 40.0 * 5.0 / 3.0
    qx, qy, qz = q * (xs - 2.0 * da), q * (ys - 2.0 * db), q * (zs - 2.0 * dc)
    m = 1.98 / 8.0
    mx, my, mz = m * (xde - xfg), m * (yhi - yde), m * (zfg - zhi)
    b1, b2 = -11.0 * ae - 4.0 * ap, 8.0 * ae + ap
    bm, cm, bs, cs = b - 2.0 * bp, c - 2.0 * cp, b + bp, c + cp
    b1m = b1 - bm
    exy, exz, eyz = b2 + bs + cs, b2 + bs - cs, b2 - 2.0 * bs
    even = [b1m + 3.0 * bm, b1m + cm, b1m - cm, exy + dxy, exy - dxy, exz + dxz, exz - dxz, eyz + dyz, eyz - dyz]
    warmth = g[0] + (g[1] + g[2]) + (g[3] + g[4]) + (g[5] + g[6])
    push = (EXPANSION / 6.0) * (warmth - 1.0)
    half = 0.5 * push
    xp, xm, yp, ym, zp, zm = qx + mx, qx - mx, qy + my, qy - my, qz + mz - half, qz - mz - half
    odd = [-4.0 * qx, -4.0 * qy, -4.0 * qz - push, xp + ym, xp - ym, xm + zp, xm - zp, yp + zm, yp - zm]
    post = [f[0] + 30.0 * ae - 12.0 * ap]
    for k in range(9):
        post.append(f[2 * k + 1] - (even[k] + odd[k]))
        post.append(f[2 * k + 2] - (even[k] - odd[k]))
    keep = 1.0 - rate
    rest = 0.125 * (rate * warmth + heat)
    half_rate = 0.5 * rate * warmth
    post.append(keep * g[0] + 2.0 * rest)
    for k, u in enumerate((ux, uy, uz)):
        move = half_rate * u
        post.append(keep * g[2 * k + 1] + (rest + move))
        post.append(keep * g[2 * k + 2] + (rest - move))
    frac = jnp.where(kind == 1, mass * inv, jnp.where(kind == 2, 1.0, 0.0))
    return post, frac, (ux, uy, uz)


def kernel(gx_size, gy_size, *refs):
    flow_in, heat_in, mass_in, diff_in, source_in, kind_in, mask_in = refs[:7]
    flow_out, heat_out, mass_out = refs[7:10]
    (flow, warm, mass, rate, source, kinds, masks, post, vel, own_frac, t_buf, y_buf, h_buf, code, liquid, shared,
     load_sem, send_sem, recv_sem) = refs[10:]
    gx, gy = lax.axis_index("gx"), lax.axis_index("gy")

    def there(dx, dy):
        tests = []
        if dx:
            tests.append(gx < gx_size - 1 if dx > 0 else gx > 0)
        if dy:
            tests.append(gy < gy_size - 1 if dy > 0 else gy > 0)
        return functools.reduce(jnp.logical_and, tests)

    loads = [
        pltpu.make_async_copy(src, dst, load_sem.at[i])
        for i, (src, dst) in enumerate(
            [(flow_in, flow), (heat_in, warm), (mass_in, mass), (diff_in, rate), (source_in, source), (kind_in, kinds),
             (mask_in, masks)]
        )
    ]
    for load in loads:
        load.start()
    barrier = pltpu.get_barrier_semaphore()
    for dx, dy in CLASSES:

        @pl.when(there(dx, dy))
        def _():
            pl.semaphore_signal(barrier, inc=1, device_id=(gx + dx, gy + dy), device_id_type=MESH)

    def copy_of(rd, cls):
        dx, dy = CLASSES[cls]
        first = rd == 0
        if not dy:
            own, far = (ROWS, 0) if dx > 0 else (1, ROWS + 1)
            if dx > 0:
                fields = pl.ds(0, 8 if first else 7)
            else:
                fields = pl.ds(7 if first else 6, 8 if first else 7)
            src, dst = t_buf.at[rd, fields, own], t_buf.at[rd, fields, far]
        else:
            side, edge = (0, 0) if dy > 0 else (1, SUB - 1)
            line = pl.ds(edge, 1)
            if not dx:
                fields = pl.ds(0, 8 if first else 7)
                own = far = pl.ds(1, ROWS)
            elif dx > 0:
                fields = pl.ds(4, 3 if first else 2)
                own, far = ROWS, 0
            else:
                fields = pl.ds(6 if first else 5, 3 if first else 2)
                own, far = 1, ROWS + 1
            src, dst = y_buf.at[rd, side, fields, own, line], h_buf.at[rd, side, fields, far, line]
        return pltpu.make_async_remote_copy(
            src_ref=src,
            dst_ref=dst,
            send_sem=send_sem.at[rd, cls],
            recv_sem=recv_sem.at[rd, cls],
            device_id=(gx + dx, gy + dy),
            device_id_type=MESH,
        )

    def send(rd, classes):
        for cls in classes:

            @pl.when(there(*CLASSES[cls]))
            def _():
                copy_of(rd, cls).start()

    def receive(rd, classes):
        for cls in classes:
            dx, dy = CLASSES[cls]

            @pl.when(there(-dx, -dy))
            def _():
                copy_of(rd, cls).wait_recv()

    line_of = lax.broadcasted_iota(jnp.int32, (SUB, LANE), 0)
    edge_of = {1: line_of == 0, -1: line_of == SUB - 1}
    top = lax.broadcasted_iota(jnp.int32, (SUB, LANE), 1) == LANE - 1

    def collide_row(rd, r, f, g, m):
        kind = kinds[r]
        if rd == 0:
            rate[r] = 1.0 / (0.5 + 4.0 * rate[r])
        values, frac, velocity = collide(f, g, m, rate[r], source[r], kind)
        for i in range(26):
            post[i, r] = values[i]
        for i in range(3):
            vel[i, r] = velocity[i]
        own_frac[r] = frac
        fields = dict(enumerate(values))
        fields[FRAC] = frac
        if rd == 0:
            fields[KIND_A] = fields[KIND_B] = kind.astype(jnp.float32)
        moved = {}
        for i, field in enumerate(X_FIELDS[min(rd, 1)]):
            value = fields[field]
            if field < 26:
                dx, dy, dz = VELOCITY[field if field < 19 else field - 19]
                value = moved[field] = roll_y(roll_z(value, dz), dy)
            t_buf[rd, i, r + 1] = value
        for side, way in ((0, 1), (1, -1)):
            for i, field in enumerate(Y_FIELDS[min(rd, 1)][way]):
                if field in moved:
                    value = moved[field]
                else:
                    dz = VELOCITY[field if field < 19 else field - 19][2] if field < 26 else 0
                    value = roll_y(roll_z(fields[field], dz), way)
                y_buf[rd, side, i, r + 1] = value

    def joined(rd, way, field, row, value):
        side, edge = (0, 0) if way > 0 else (1, SUB - 1)
        return jnp.where(edge_of[way], h_buf[rd, side, y_index(rd, way, field), row, edge : edge + 1], value)

    def sources(rd, r, field_of, own):
        plain = {0: own, 1: field_of(r), -1: field_of(r + 2)}
        found = {}
        for dx in (0, 1, -1):
            row = r + 1 - dx
            found[dx, 0] = plain[dx]
            for way in (1, -1):
                if isinstance(field_of.name, dict):
                    name = field_of.name[dx]
                else:
                    name = field_of.name
                found[dx, way] = joined(rd, way, name, row, roll_y(plain[dx], way))
        return {i: roll_z(found[VELOCITY[i][0], VELOCITY[i][1]], VELOCITY[i][2]) for i in range(1, 19)}

    def stream_row(rd, r, last_row):
        kind = kinds[r]
        if rd == 0:

            def kind_at(row):
                return t_buf[rd, x_index(rd, KIND_B if last_row and row is not r else KIND_A), row]

            kind_at.name = {0: KIND_A, 1: KIND_A, -1: KIND_B if last_row else KIND_A}
            kind_from = sources(rd, r, kind_at, kind.astype(jnp.float32))

        def frac_at(row):
            return t_buf[rd, x_index(rd, FRAC), row]

        frac_at.name = FRAC
        frac = own_frac[r]
        frac_from = sources(rd, r, frac_at, frac)
        ux, uy, uz = vel[0, r], vel[1, r], vel[2, r]
        base = 2.0 - 3.0 * (ux * ux + uy * uy + uz * uz)
        old = [post[i, r] for i in range(26)]

        def incoming(i):
            dx, dy, dz = VELOCITY[i if i < 19 else i - 19]
            row = r + 1 - dx
            if dx == 0 and dy == 0:
                return roll_z(old[i], dz)
            if dx and not dy:
                return t_buf[rd, x_index(rd, i), row]
            if dx:
                return joined(rd, dy, i, row, t_buf[rd, x_index(rd, i), row])
            return joined(rd, dy, i, row, y_buf[rd, 0 if dy > 0 else 1, y_index(rd, dy, i), row])

        f_new, g_new = [old[0]], [old[19]]
        change = jnp.zeros((SUB, LANE), jnp.float32)
        closed = {}
        for i in range(1, 19):
            if rd == 0:
                word = masks[(i - 1) // 9, r]
                enabled = ((word >> ((i - 1) % 9)) & 1).astype(jnp.float32)
                here = kind_from[i]
                if VELOCITY[i][2] < 0:
                    here = jnp.where(top, 0.0, here)
                code[i - 1, r] = here
                whole = jnp.where(here == 2.0, enabled, 0.0)
                part = jnp.where(here == 1.0, 0.5 * enabled, 0.0)
                liquid[i - 1, r] = whole
                shared[i - 1, r] = part
            else:
                here, whole, part = code[i - 1, r], liquid[i - 1, r], shared[i - 1, r]
            wall, gas = here == 3.0, here == 0.0
            dx, dy, dz = VELOCITY[i]
            along = sum(s * u for s, u in zip((dx, dy, dz), (ux, uy, uz)) if s)
            rebuilt = WEIGHTS[i] * (base + 9.0 * (along * along))
            arriving, back = incoming(i), old[OPPOSITE[i]]
            f_new.append(jnp.where(wall, back, jnp.where(gas, rebuilt - back, arriving)))
            change = change + (whole + part * (frac + frac_from[i])) * (arriving - back)
            if i < 7:
                closed[i] = jnp.logical_or(wall, gas)
        for k in range(1, 7):
            g_new.append(jnp.where(closed[k], old[19 + OPPOSITE[k]], incoming(19 + k)))
        fluid = jnp.logical_or(kind == 1, kind == 2)
        f_new = [jnp.where(fluid, f_new[i], flow[i, r]) for i in range(19)]
        g_new = [jnp.where(fluid, g_new[k], warm[k, r]) for k in range(7)]
        total = functools.reduce(jnp.add, f_new)
        m_new = jnp.where(kind == 1, mass[r] + change, jnp.where(kind == 2, total, 0.0))
        if rd == ITERS - 1:
            for i in range(19):
                flow_out[i, r] = f_new[i]
            for k in range(7):
                heat_out[k, r] = g_new[k]
            mass_out[r] = m_new
            return
        for i in range(19):
            flow[i, r] = f_new[i]
        for k in range(7):
            warm[k, r] = g_new[k]
        mass[r] = m_new
        collide_row(rd + 1, r, f_new, g_new, m_new)

    def first_row(r):
        collide_row(0, r, [flow[i, r] for i in range(19)], [warm[k, r] for k in range(7)], mass[r])

    for load in loads[:6]:
        load.wait()
    first_row(0)
    first_row(ROWS - 1)
    pl.semaphore_wait(barrier, sum(there(dx, dy).astype(jnp.int32) for dx, dy in CLASSES))
    send(0, range(6))
    lax.fori_loop(1, ROWS - 1, lambda r, _: (first_row(r), 0)[1], 0)
    send(0, (6, 7))
    loads[6].wait()
    for rd in range(ITERS):
        receive(rd, (6, 7))
        lax.fori_loop(1, ROWS - 1, lambda r, _: (stream_row(rd, r, False), 0)[1], 0)
        receive(rd, (0, 2, 3))
        stream_row(rd, 0, False)
        if rd < ITERS - 1:
            send(rd + 1, (1, 4, 5))
        receive(rd, (1, 4, 5))
        stream_row(rd, ROWS - 1, True)
        if rd < ITERS - 1:
            send(rd + 1, (0, 2, 3))
            send(rd + 1, (6, 7))
    for cls in range(8):

        @pl.when(there(*CLASSES[cls]))
        def _():
            for rd in range(ITERS):
                copy_of(rd, cls).wait_send()


def write_out(*refs):
    sem = refs[6]
    copies = [pltpu.make_async_copy(refs[i], refs[3 + i], sem.at[i]) for i in range(3)]
    for copy in copies:
        copy.start()
    for copy in copies:
        copy.wait()


def solution(mesh):
    gx_size, gy_size = mesh.shape["gx"], mesh.shape["gy"]
    f32, i32 = jnp.float32, jnp.int32
    row = (ROWS, SUB, LANE)
    shapes = [(19,) + row, (7,) + row, row]
    in_vmem = pl.BlockSpec(memory_space=pltpu.VMEM)
    in_hbm = pl.BlockSpec(memory_space=pltpu.HBM)

    def shards(*args):
        halo = (ITERS, 2, 9, ROWS + 2, SUB, LANE)
        done = pl.pallas_call(
            functools.partial(kernel, gx_size, gy_size),
            out_shape=[pltpu.VMEM(s, f32) for s in shapes],
            in_specs=[in_hbm] * 7,
            out_specs=[in_vmem] * 3,
            scratch_shapes=[
                pltpu.VMEM((19,) + row, f32),
                pltpu.VMEM((7,) + row, f32),
                pltpu.VMEM(row, f32),
                pltpu.VMEM(row, f32),
                pltpu.VMEM(row, f32),
                pltpu.VMEM(row, i32),
                pltpu.VMEM((2,) + row, i32),
                pltpu.VMEM((26,) + row, f32),
                pltpu.VMEM((3,) + row, f32),
                pltpu.VMEM(row, f32),
                pltpu.VMEM((ITERS, 15, ROWS + 2, SUB, LANE), f32),
                pltpu.VMEM(halo, f32),
                pltpu.VMEM(halo, f32),
                pltpu.VMEM((18,) + row, f32),
                pltpu.VMEM((18,) + row, f32),
                pltpu.VMEM((18,) + row, f32),
                pltpu.SemaphoreType.DMA((7,)),
                pltpu.SemaphoreType.DMA((ITERS, 8)),
                pltpu.SemaphoreType.DMA((ITERS, 8)),
            ],
            compiler_params=pltpu.CompilerParams(
                collective_id=0, has_side_effects=True, vmem_limit_bytes=24 * 1024 * 1024
            ),
        )(*args)
        done = [pltpu.with_memory_space_constraint(a, pltpu.VMEM) for a in done]
        return tuple(
            pl.pallas_call(
                write_out,
                out_shape=[jax.ShapeDtypeStruct(s, f32) for s in shapes],
                in_specs=[in_vmem] * 3,
                out_specs=[in_hbm] * 3,
                scratch_shapes=[pltpu.SemaphoreType.DMA((3,))],
            )(*done)
        )

    block, field = P("gx", "gy", None), P(None, "gx", "gy", None)
    return jax.shard_map(
        shards,
        mesh=mesh,
        in_specs=(field, field, block, block, block, block, field),
        out_specs=(field, field, block),
        check_vma=False,
    )
```

time: 154 us -> 34.5 us (0.22)
  starting transfers between devices: 109 us -> 0 us
  Pallas kernels: 0 us -> 27.7 us
  waiting for transfers between devices: 18.7 us -> 0 us
  other arithmetic: 14.1 us -> 0 us
  matrix products: 2.12 us -> 0 us
  between operations: 2.74 us -> 0.66 us
    ppermute x28 -> x0, starting transfers between devices: 109 us -> none  [the longest x14 70.4 us: padded_2(): lax.ppermute(lax.slice_in_dim(block, 0, width, axis=dim), axis, backward)]
    pallas_call x0 -> x2, Pallas kernels: none -> 27.7 us  [the longest x1 26.9 us: shards(): pl.pallas_call(functools.partial(kernel, gx_size, gy_size), out_shape=[pl...]
    ppermute x28 -> x0, waiting for transfers between devices: 18.7 us -> none  [the longest x14 16.4 us: padded_2(): lax.ppermute(lax.slice_in_dim(block, 0, width, axis=dim), axis, backward)]
    unnamed x194 -> x0, other arithmetic: 5.41 us -> none
    slice x55 -> x0, local copies, waits for them, and re-layouts: 4.12 us -> none  [the longest x20 1.49 us: shift_depth(): values[..., 1:]]
    unnamed x21 -> x14, local copies, waits for them, and re-layouts: 2.13 us -> 5.68 us
    broadcast_in_dim x3 -> x0, other arithmetic: 2.17 us -> none  [shards(): fill_frac[None]]
    dot_general x3 -> x0, matrix products: 2.12 us -> none  [collision(): jnp.einsum('ij,jxyz->ixyz', kernel, flow_pops - balance, precision=lax.Pr...]
  transfers between devices with their start and end apart: 28 -> 0, of which waited for: 7 -> 0; matrix products, arithmetic and copies ran while one was open for 6% -> 0% of each run, Pallas kernels for 0% -> 0%
where the time goes in v1:
time: 34.5 us; the launch traced here: 34 us
  Pallas kernels  27.7 us (80%)
  local copies, waits for them, and re-layouts  5.68 us (16%)
  between operations  0.66 us (2%)
    pallas_call x1, Pallas kernels, shards(): pl.pallas_call(functools.partial(kernel, gx_size, gy_size), out_shape=[pl...  26.9 us
    unnamed x14, local copies, waits for them, and re-layouts  5.68 us
    pallas_call x1, Pallas kernels, shards(): pl.pallas_call(write_out, out_shape=[jax.ShapeDtypeStruct(s, f32) for s i...  0.85 us

profile of v1, /device:TPU:7, one launch (start us, length us, event | category | flops | bytes accessed | tf_op | source)
XLA Modules:
  0.0 34.0 jit_solution(8742359755790300292)
XLA Ops:
  0.6 0.0 copy-start
  0.6 1.0 %copy-done = f32[19,6,8,128]{3,2,1,0:T(8,128)S(1)} copy-done((f32[19,6,8,128]{3,2,1,0:T(8,128)S(1)}, f32[19,6,8,128]{3,2,1,0:T(8,128)}, u32[]{:S(2)}) %copy-start) | copy-done | bytes 466968
  1.7 0.0 copy-start.1
  1.7 0.9 %copy-done.1 = f32[7,6,8,128]{3,2,1,0:T(8,128)S(1)} copy-done((f32[7,6,8,128]{3,2,1,0:T(8,128)S(1)}, f32[7,6,8,128]{3,2,1,0:T(8,128)}, u32[]{:S(2)}) %copy-start.1) | copy-done | bytes 172056
  2.6 0.0 copy-start.2
  2.6 0.8 %copy-done.2 = s32[2,6,8,128]{3,2,1,0:T(8,128)S(1)} copy-done((s32[2,6,8,128]{3,2,1,0:T(8,128)S(1)}, s32[2,6,8,128]{3,2,1,0:T(8,128)}, u32[]{:S(2)}) %copy-start.2) | copy-done | bytes 49176
  3.4 0.0 copy-start.3
  3.4 0.7 %copy-done.3 = f32[6,8,128]{2,1,0:T(8,128)S(1)} copy-done((f32[6,8,128]{2,1,0:T(8,128)S(1)}, f32[6,8,128]{2,1,0:T(8,128)}, u32[]{:S(2)}) %copy-start.3) | copy-done | bytes 24600
  4.1 0.0 copy-start.4
  4.1 0.7 %copy-done.4 = f32[6,8,128]{2,1,0:T(8,128)S(1)} copy-done((f32[6,8,128]{2,1,0:T(8,128)S(1)}, f32[6,8,128]{2,1,0:T(8,128)}, u32[]{:S(2)}) %copy-start.4) | copy-done | bytes 24600
  4.8 0.0 copy-start.5
  4.9 0.7 %copy-done.5 = f32[6,8,128]{2,1,0:T(8,128)S(1)} copy-done((f32[6,8,128]{2,1,0:T(8,128)S(1)}, f32[6,8,128]{2,1,0:T(8,128)}, u32[]{:S(2)}) %copy-start.5) | copy-done | bytes 24600
  5.6 0.0 copy-start.6
  5.6 0.7 %copy-done.6 = s32[6,8,128]{2,1,0:T(8,128)S(1)} copy-done((s32[6,8,128]{2,1,0:T(8,128)S(1)}, s32[6,8,128]{2,1,0:T(8,128)}, u32[]{:S(2)}) %copy-start.6) | copy-done | bytes 24600
  6.3 26.9 %shard_map.94 = (f32[19,6,8,128]{3,2,1,0:T(8,128)S(1)}, f32[7,6,8,128]{3,2,1,0:T(8,128)S(1)}, f32[6,8,128]{2,1,0:T(8,128)S(1)}) custom-call(f32[19,6,8,128]{3,2,1,0:T(8,128)S(1)} %copy-done, f32[7,6,8,128]{3,2,1,0:T(8,128)S(1)} %copy-done.1, f32[6,8,128]{2,1,0:T(8,128)S(1)} %copy-done.3, f32[6,8,128]{2,1,0:T(8,128)S(1)} %copy-done.4, ...), custom_call_target="tpu_custom_call" | custom-call | tf_op jit(solution)/shard_map/pallas_call | solution.py:384
  33.2 0.9 %shard_map.95 = (f32[19,6,8,128]{3,2,1,0:T(8,128)}, f32[7,6,8,128]{3,2,1,0:T(8,128)}, f32[6,8,128]{2,1,0:T(8,128)}) custom-call(f32[19,6,8,128]{3,2,1,0:T(8,128)S(1)} %get-tuple-element.6.refs_0_, f32[7,6,8,128]{3,2,1,0:T(8,128)S(1)} %get-tuple-element.7.refs_1_, f32[6,8,128]{2,1,0:T(8,128)S(1)} %get-tuple-element.8.refs_2_), custom_call_target="tpu_custom_call" | custom-call | tf_op jit(solution)/shard_map/pallas_call | solution.py:416
Async XLA Ops:
  0.6 1.0 %copy-start = (f32[19,6,8,128]{3,2,1,0:T(8,128)S(1)}, f32[19,6,8,128]{3,2,1,0:T(8,128)}, u32[]{:S(2)}) copy-start(f32[19,6,8,128]{3,2,1,0:T(8,128)} %refs_0_.1) | copy-start | bytes 1400836
  1.7 0.9 %copy-start.1 = (f32[7,6,8,128]{3,2,1,0:T(8,128)S(1)}, f32[7,6,8,128]{3,2,1,0:T(8,128)}, u32[]{:S(2)}) copy-start(f32[7,6,8,128]{3,2,1,0:T(8,128)} %refs_1_.1) | copy-start | bytes 516100
  2.6 0.8 %copy-start.2 = (s32[2,6,8,128]{3,2,1,0:T(8,128)S(1)}, s32[2,6,8,128]{3,2,1,0:T(8,128)}, u32[]{:S(2)}) copy-start(s32[2,6,8,128]{3,2,1,0:T(8,128)} %refs_6_.1) | copy-start | bytes 147460
  3.4 0.7 %copy-start.3 = (f32[6,8,128]{2,1,0:T(8,128)S(1)}, f32[6,8,128]{2,1,0:T(8,128)}, u32[]{:S(2)}) copy-start(f32[6,8,128]{2,1,0:T(8,128)} %refs_2_.1) | copy-start | bytes 73732
  4.1 0.7 %copy-start.4 = (f32[6,8,128]{2,1,0:T(8,128)S(1)}, f32[6,8,128]{2,1,0:T(8,128)}, u32[]{:S(2)}) copy-start(f32[6,8,128]{2,1,0:T(8,128)} %refs_3_.1) | copy-start | bytes 73732
  4.8 0.7 %copy-start.5 = (f32[6,8,128]{2,1,0:T(8,128)S(1)}, f32[6,8,128]{2,1,0:T(8,128)}, u32[]{:S(2)}) copy-start(f32[6,8,128]{2,1,0:T(8,128)} %refs_4_.1) | copy-start | bytes 73732
  5.6 0.7 %copy-start.6 = (s32[6,8,128]{2,1,0:T(8,128)S(1)}, s32[6,8,128]{2,1,0:T(8,128)}, u32[]{:S(2)}) copy-start(s32[6,8,128]{2,1,0:T(8,128)} %refs_5_.1) | copy-start | bytes 73732

commit v2 on v1

--- a/solution.py
+++ b/solution.py
@@ -44,7 +44,10 @@
     {1: [3, 15, 17, 22, KIND_A, 7, FRAC, 10, KIND_B], -1: [4, 16, 18, 23, KIND_A, 9, FRAC, 8, KIND_B]},
     {1: [3, 15, 17, 22, 7, FRAC, 10], -1: [4, 16, 18, 23, 9, FRAC, 8]},
 ]
-CLASSES = [(1, 0), (-1, 0), (1, 1), (1, -1), (-1, 1), (-1, -1), (0, 1), (0, -1)]
+NEIGHBOURS = [(1, 0), (-1, 0), (1, 1), (1, -1), (-1, 1), (-1, -1), (0, 1), (0, -1)]
+LOW, HIGH, INNER = (1, 1), (ROWS, 1), (2, ROWS - 2)
+CLASSES = [way + (None,) for way in NEIGHBOURS[:6]] + [(0, dy, part) for part in (LOW, HIGH, INNER) for dy in (1, -1)]
+TO_HIGH, TO_LOW, Y_LOW, Y_HIGH, Y_INNER = (0, 2, 3), (1, 4, 5), (6, 7), (8, 9), (10, 11)
 
 
 def x_index(rd, field):
@@ -137,24 +140,36 @@
             tests.append(gy < gy_size - 1 if dy > 0 else gy > 0)
         return functools.reduce(jnp.logical_and, tests)
 
-    loads = [
-        pltpu.make_async_copy(src, dst, load_sem.at[i])
-        for i, (src, dst) in enumerate(
-            [(flow_in, flow), (heat_in, warm), (mass_in, mass), (diff_in, rate), (source_in, source), (kind_in, kinds),
-             (mask_in, masks)]
-        )
-    ]
-    for load in loads:
-        load.start()
     barrier = pltpu.get_barrier_semaphore()
-    for dx, dy in CLASSES:
+    for dx, dy in NEIGHBOURS:
 
         @pl.when(there(dx, dy))
         def _():
             pl.semaphore_signal(barrier, inc=1, device_id=(gx + dx, gy + dy), device_id_type=MESH)
 
+    count = [0]
+
+    def load(*pairs):
+        started = []
+        for src, dst in pairs:
+            started.append(pltpu.make_async_copy(src, dst, load_sem.at[count[0]]))
+            count[0] += 1
+        for copy in started:
+            copy.start()
+        return started
+
+    def rows_of(at, size):
+        cut = (slice(None), pl.ds(at, size))
+        return (flow_in.at[cut], flow.at[cut]), (heat_in.at[cut], warm.at[cut])
+
+    last_loads = load(
+        *rows_of(ROWS - 1, 1), (mass_in, mass), (diff_in, rate), (source_in, source), (kind_in, kinds)
+    )
+    first_loads = load(*rows_of(0, 1))
+    inner_loads = load(*rows_of(1, ROWS - 2), (mask_in, masks))
+
     def copy_of(rd, cls):
-        dx, dy = CLASSES[cls]
+        dx, dy, part = CLASSES[cls]
         first = rd == 0
         if not dy:
             own, far = (ROWS, 0) if dx > 0 else (1, ROWS + 1)
@@ -168,7 +183,7 @@
             line = pl.ds(edge, 1)
             if not dx:
                 fields = pl.ds(0, 8 if first else 7)
-                own = far = pl.ds(1, ROWS)
+                own = far = pl.ds(*part)
             elif dx > 0:
                 fields = pl.ds(4, 3 if first else 2)
                 own, far = ROWS, 0
@@ -188,13 +203,13 @@
     def send(rd, classes):
         for cls in classes:
 
-            @pl.when(there(*CLASSES[cls]))
+            @pl.when(there(*CLASSES[cls][:2]))
             def _():
                 copy_of(rd, cls).start()
 
     def receive(rd, classes):
         for cls in classes:
-            dx, dy = CLASSES[cls]
+            dx, dy, _ = CLASSES[cls]
 
             @pl.when(there(-dx, -dy))
             def _():
@@ -333,30 +348,40 @@
     def first_row(r):
         collide_row(0, r, [flow[i, r] for i in range(19)], [warm[k, r] for k in range(7)], mass[r])
 
-    for load in loads[:6]:
-        load.wait()
+    def wait(copies):
+        for copy in copies:
+            copy.wait()
+
+    def rows_in_turn(body, first, step):
+        lax.fori_loop(0, 2, lambda k, _: (body(first + step * k), 0)[1], 0)
+
+    wait(last_loads)
+    first_row(ROWS - 1)
+    wait(first_loads)
     first_row(0)
-    first_row(ROWS - 1)
-    pl.semaphore_wait(barrier, sum(there(dx, dy).astype(jnp.int32) for dx, dy in CLASSES))
-    send(0, range(6))
+    pl.semaphore_wait(barrier, sum(there(dx, dy).astype(jnp.int32) for dx, dy in NEIGHBOURS))
+    send(0, TO_HIGH + TO_LOW + Y_LOW + Y_HIGH)
+    wait(inner_loads)
     lax.fori_loop(1, ROWS - 1, lambda r, _: (first_row(r), 0)[1], 0)
-    send(0, (6, 7))
-    loads[6].wait()
+    send(0, Y_INNER)
     for rd in range(ITERS):
-        receive(rd, (6, 7))
-        lax.fori_loop(1, ROWS - 1, lambda r, _: (stream_row(rd, r, False), 0)[1], 0)
-        receive(rd, (0, 2, 3))
-        stream_row(rd, 0, False)
-        if rd < ITERS - 1:
-            send(rd + 1, (1, 4, 5))
-        receive(rd, (1, 4, 5))
-        stream_row(rd, ROWS - 1, True)
-        if rd < ITERS - 1:
-            send(rd + 1, (0, 2, 3))
-            send(rd + 1, (6, 7))
-    for cls in range(8):
-
-        @pl.when(there(*CLASSES[cls]))
+        more = rd < ITERS - 1
+        receive(rd, Y_INNER)
+        rows_in_turn(lambda r: stream_row(rd, r, False), 2, 1)
+        ends = [(0, 1, TO_HIGH + Y_LOW, TO_LOW + Y_LOW), (ROWS - 1, ROWS - 2, TO_LOW + Y_HIGH, TO_HIGH + Y_HIGH)]
+        for r, beside, needed, leaving in ends if more else reversed(ends):
+            receive(rd, needed)
+            stream_row(rd, r, r == ROWS - 1)
+            if more:
+                send(rd + 1, leaving)
+            else:
+                stream_row(rd, beside, False)
+        if more:
+            rows_in_turn(lambda r: stream_row(rd, r, False), 1, ROWS - 3)
+            send(rd + 1, Y_INNER)
+    for cls in range(len(CLASSES)):
+
+        @pl.when(there(*CLASSES[cls][:2]))
         def _():
             for rd in range(ITERS):
                 copy_of(rd, cls).wait_send()
@@ -403,14 +428,14 @@
                 pltpu.VMEM((18,) + row, f32),
                 pltpu.VMEM((18,) + row, f32),
                 pltpu.VMEM((18,) + row, f32),
-                pltpu.SemaphoreType.DMA((7,)),
-                pltpu.SemaphoreType.DMA((ITERS, 8)),
-                pltpu.SemaphoreType.DMA((ITERS, 8)),
+                pltpu.SemaphoreType.DMA((11,)),
+                pltpu.SemaphoreType.DMA((ITERS, len(CLASSES))),
+                pltpu.SemaphoreType.DMA((ITERS, len(CLASSES))),
             ],
             compiler_params=pltpu.CompilerParams(
                 collective_id=0, has_side_effects=True, vmem_limit_bytes=24 * 1024 * 1024
             ),
-        )(*args)
+        )(*[pltpu.with_memory_space_constraint(a, pltpu.HBM) for a in args])
         done = [pltpu.with_memory_space_constraint(a, pltpu.VMEM) for a in done]
         return tuple(
             pl.pallas_call(

time: 34.5 us -> 27.6 us (0.80)
  local copies, waits for them, and re-layouts: 5.68 us -> 0 us
  Pallas kernels: 27.7 us -> 26.8 us
    unnamed x14 -> x0, local copies, waits for them, and re-layouts: 5.68 us -> none
    pallas_call x1, Pallas kernels: 26.9 us -> 25.9 us  [shards(): pl.pallas_call(functools.partial(kernel, gx_size, gy_size), out_shape=[pl...]
where the time goes in v2:
time: 27.6 us; the launch traced here: 27.4 us
  Pallas kernels  26.8 us (97%)
  between operations  0.64 us (2%)
    pallas_call x1, Pallas kernels, shards(): pl.pallas_call(functools.partial(kernel, gx_size, gy_size), out_shape=[pl...  25.9 us
    pallas_call x1, Pallas kernels, shards(): pl.pallas_call(write_out, out_shape=[jax.ShapeDtypeStruct(s, f32) for s i...  0.85 us

profile of v2, /device:TPU:7, one launch (start us, length us, event | category | flops | bytes accessed | tf_op | source)
XLA Modules:
  0.0 27.4 jit_solution(17358521570424960942)
XLA Ops:
  0.6 25.9 %shard_map.94 = (f32[19,6,8,128]{3,2,1,0:T(8,128)S(1)}, f32[7,6,8,128]{3,2,1,0:T(8,128)S(1)}, f32[6,8,128]{2,1,0:T(8,128)S(1)}) custom-call(f32[19,6,8,128]{3,2,1,0:T(8,128)} %refs_0_.1, f32[7,6,8,128]{3,2,1,0:T(8,128)} %refs_1_.1, f32[6,8,128]{2,1,0:T(8,128)} %refs_2_.1, f32[6,8,128]{2,1,0:T(8,128)} %refs_3_.1, f32[6,8,128]{2,1,0:T(8,128)} %refs_4_.1, ...), custom_call_target="tpu_custom_call" | custom-call | tf_op jit(solution)/shard_map/pallas_call | solution.py:409
  26.6 0.9 %shard_map.95 = (f32[19,6,8,128]{3,2,1,0:T(8,128)}, f32[7,6,8,128]{3,2,1,0:T(8,128)}, f32[6,8,128]{2,1,0:T(8,128)}) custom-call(f32[19,6,8,128]{3,2,1,0:T(8,128)S(1)} %get-tuple-element.6.refs_0_, f32[7,6,8,128]{3,2,1,0:T(8,128)S(1)} %get-tuple-element.7.refs_1_, f32[6,8,128]{2,1,0:T(8,128)S(1)} %get-tuple-element.8.refs_2_), custom_call_target="tpu_custom_call" | custom-call | tf_op jit(solution)/shard_map/pallas_call | solution.py:441

commit v3 on v2

--- a/solution.py
+++ b/solution.py
@@ -36,6 +36,7 @@
 ROWS, SUB, LANE = 6, 8, 128
 
 FRAC, KIND_A, KIND_B = 26, 27, 28
+MASS, RATE, SOURCE = 26, 27, 28
 X_FIELDS = [
     [KIND_A, 1, 7, 9, 11, 13, 20, FRAC, 2, 8, 10, 12, 14, 21, KIND_B],
     [1, 7, 9, 11, 13, 20, FRAC, 2, 8, 10, 12, 14, 21],
@@ -47,7 +48,8 @@
 NEIGHBOURS = [(1, 0), (-1, 0), (1, 1), (1, -1), (-1, 1), (-1, -1), (0, 1), (0, -1)]
 LOW, HIGH, INNER = (1, 1), (ROWS, 1), (2, ROWS - 2)
 CLASSES = [way + (None,) for way in NEIGHBOURS[:6]] + [(0, dy, part) for part in (LOW, HIGH, INNER) for dy in (1, -1)]
-TO_HIGH, TO_LOW, Y_LOW, Y_HIGH, Y_INNER = (0, 2, 3), (1, 4, 5), (6, 7), (8, 9), (10, 11)
+GROUPS = [(0, 2, 3), (1, 4, 5), (6, 7), (8, 9), (10, 11)]
+TO_HIGH, TO_LOW, Y_LOW, Y_HIGH, Y_INNER = range(5)
 
 
 def x_index(rd, field):
@@ -64,6 +66,13 @@
 
 def roll_z(value, dz):
     return pltpu.roll(value, dz % LANE, 1) if dz else value
+
+
+def tree(terms):
+    terms = list(terms)
+    while len(terms) > 1:
+        terms = [sum(terms[i : i + 2][1:], terms[i]) for i in range(0, len(terms), 2)]
+    return terms[0]
 
 
 def collide(f, g, mass, rate, heat, kind):
@@ -128,7 +137,7 @@
 def kernel(gx_size, gy_size, *refs):
     flow_in, heat_in, mass_in, diff_in, source_in, kind_in, mask_in = refs[:7]
     flow_out, heat_out, mass_out = refs[7:10]
-    (flow, warm, mass, rate, source, kinds, masks, post, vel, own_frac, t_buf, y_buf, h_buf, code, liquid, shared,
+    (state, kinds, masks, post, vel, own_frac, t_buf, y_buf, h_buf, code, liquid, shared, t_size,
      load_sem, send_sem, recv_sem) = refs[10:]
     gx, gy = lax.axis_index("gx"), lax.axis_index("gy")
 
@@ -147,29 +156,30 @@
         def _():
             pl.semaphore_signal(barrier, inc=1, device_id=(gx + dx, gy + dy), device_id_type=MESH)
 
-    count = [0]
-
-    def load(*pairs):
-        started = []
-        for src, dst in pairs:
-            started.append(pltpu.make_async_copy(src, dst, load_sem.at[count[0]]))
-            count[0] += 1
-        for copy in started:
-            copy.start()
-        return started
-
-    def rows_of(at, size):
-        cut = (slice(None), pl.ds(at, size))
-        return (flow_in.at[cut], flow.at[cut]), (heat_in.at[cut], warm.at[cut])
-
-    last_loads = load(
-        *rows_of(ROWS - 1, 1), (mass_in, mass), (diff_in, rate), (source_in, source), (kind_in, kinds)
-    )
-    first_loads = load(*rows_of(0, 1))
-    inner_loads = load(*rows_of(1, ROWS - 2), (mask_in, masks))
+    def rows_of(at, size, sem):
+        rows = pl.ds(at, size)
+        return [
+            pltpu.make_async_copy(flow_in.at[:, rows], state.at[pl.ds(0, 19), rows], load_sem.at[sem]),
+            pltpu.make_async_copy(heat_in.at[:, rows], state.at[pl.ds(19, 7), rows], load_sem.at[sem]),
+        ]
+
+    def wait_rows(at, size, sem):
+        there = state.at[pl.ds(0, 26), pl.ds(at, size)]
+        pltpu.make_async_copy(there, there, load_sem.at[sem]).wait()
+
+    load_kinds = pltpu.make_async_copy(kind_in, kinds, load_sem.at[3])
+    load_masks = pltpu.make_async_copy(mask_in, masks, load_sem.at[4])
+    load_cells = [
+        pltpu.make_async_copy(src, state.at[at], load_sem.at[5])
+        for src, at in ((mass_in, MASS), (diff_in, RATE), (source_in, SOURCE))
+    ]
+    for load in rows_of(ROWS - 1, 1, 0) + load_cells + [load_kinds] + rows_of(0, 1, 1) + rows_of(1, ROWS - 2, 2):
+        load.start()
+    load_masks.start()
 
     def copy_of(rd, cls):
         dx, dy, part = CLASSES[cls]
+        group = [cls in members for members in GROUPS].index(True)
         first = rd == 0
         if not dy:
             own, far = (ROWS, 0) if dx > 0 else (1, ROWS + 1)
@@ -194,26 +204,41 @@
         return pltpu.make_async_remote_copy(
             src_ref=src,
             dst_ref=dst,
-            send_sem=send_sem.at[rd, cls],
-            recv_sem=recv_sem.at[rd, cls],
+            send_sem=send_sem.at[rd % 2, group],
+            recv_sem=recv_sem.at[rd % 2, group],
             device_id=(gx + dx, gy + dy),
             device_id_type=MESH,
         )
 
-    def send(rd, classes):
-        for cls in classes:
-
-            @pl.when(there(*CLASSES[cls][:2]))
+    def send(rd, *groups):
+        for group in groups:
+            for cls in GROUPS[group]:
+
+                @pl.when(there(*CLASSES[cls][:2]))
+                def _():
+                    copy_of(rd, cls).start()
+
+    def wait_group(rd, group, sem, there_x):
+        fields = 8 if rd == 0 else 7
+        fixed, each = (fields * SUB, fields - 5) if group < 2 else (0, fields * CLASSES[GROUPS[group][0]][2][1])
+        inside = jnp.logical_and(gy > 0, gy < gy_size - 1)
+        for both in (True, False):
+            test = inside if both else jnp.logical_not(inside)
+
+            @pl.when(jnp.logical_and(test, there_x) if group < 2 else test)
             def _():
-                copy_of(rd, cls).start()
-
-    def receive(rd, classes):
-        for cls in classes:
-            dx, dy, _ = CLASSES[cls]
-
-            @pl.when(there(-dx, -dy))
-            def _():
-                copy_of(rd, cls).wait_recv()
+                lines = t_size.at[pl.ds(0, fixed + each * (2 if both else 1))]
+                pltpu.make_async_copy(lines, lines, sem).wait()
+
+    def drain(rd):
+        for group in range(len(GROUPS)):
+            wait_group(rd, group, send_sem.at[rd % 2, group], there(CLASSES[GROUPS[group][0]][0], 0) if group < 2 else None)
+
+    def receive(rd, *groups):
+        for group in groups:
+            wait_group(
+                rd, group, recv_sem.at[rd % 2, group], there(-CLASSES[GROUPS[group][0]][0], 0) if group < 2 else None
+            )
 
     line_of = lax.broadcasted_iota(jnp.int32, (SUB, LANE), 0)
     edge_of = {1: line_of == 0, -1: line_of == SUB - 1}
@@ -222,8 +247,8 @@
     def collide_row(rd, r, f, g, m):
         kind = kinds[r]
         if rd == 0:
-            rate[r] = 1.0 / (0.5 + 4.0 * rate[r])
-        values, frac, velocity = collide(f, g, m, rate[r], source[r], kind)
+            state[RATE, r] = 1.0 / (0.5 + 4.0 * state[RATE, r])
+        values, frac, velocity = collide(f, g, m, state[RATE, r], state[SOURCE, r], kind)
         for i in range(26):
             post[i, r] = values[i]
         for i in range(3):
@@ -253,39 +278,25 @@
         side, edge = (0, 0) if way > 0 else (1, SUB - 1)
         return jnp.where(edge_of[way], h_buf[rd, side, y_index(rd, way, field), row, edge : edge + 1], value)
 
-    def sources(rd, r, field_of, own):
-        plain = {0: own, 1: field_of(r), -1: field_of(r + 2)}
-        found = {}
-        for dx in (0, 1, -1):
-            row = r + 1 - dx
-            found[dx, 0] = plain[dx]
-            for way in (1, -1):
-                if isinstance(field_of.name, dict):
-                    name = field_of.name[dx]
-                else:
-                    name = field_of.name
-                found[dx, way] = joined(rd, way, name, row, roll_y(plain[dx], way))
-        return {i: roll_z(found[VELOCITY[i][0], VELOCITY[i][1]], VELOCITY[i][2]) for i in range(1, 19)}
-
-    def stream_row(rd, r, last_row):
+    def stream_row(rd, r, stages):
         kind = kinds[r]
-        if rd == 0:
-
-            def kind_at(row):
-                return t_buf[rd, x_index(rd, KIND_B if last_row and row is not r else KIND_A), row]
-
-            kind_at.name = {0: KIND_A, 1: KIND_A, -1: KIND_B if last_row else KIND_A}
-            kind_from = sources(rd, r, kind_at, kind.astype(jnp.float32))
-
-        def frac_at(row):
-            return t_buf[rd, x_index(rd, FRAC), row]
-
-        frac_at.name = FRAC
         frac = own_frac[r]
-        frac_from = sources(rd, r, frac_at, frac)
         ux, uy, uz = vel[0, r], vel[1, r], vel[2, r]
         base = 2.0 - 3.0 * (ux * ux + uy * uy + uz * uz)
+        fluid = jnp.logical_or(kind == 1, kind == 2)
         old = [post[i, r] for i in range(26)]
+        known = {}
+
+        def at_source(i, field, own):
+            dx, dy, dz = VELOCITY[i]
+            if (field, dx, dy) not in known:
+                row = r + 1 - dx
+                name = field
+                if field == KIND_A and dx == -1 and isinstance(r, int) and r == ROWS - 1:
+                    name = KIND_B
+                value = t_buf[rd, x_index(rd, name), row] if dx else own
+                known[field, dx, dy] = joined(rd, dy, name, row, roll_y(value, dy)) if dy else value
+            return roll_z(known[field, dx, dy], dz)
 
         def incoming(i):
             dx, dy, dz = VELOCITY[i if i < 19 else i - 19]
@@ -298,39 +309,36 @@
                 return joined(rd, dy, i, row, t_buf[rd, x_index(rd, i), row])
             return joined(rd, dy, i, row, y_buf[rd, 0 if dy > 0 else 1, y_index(rd, dy, i), row])
 
-        f_new, g_new = [old[0]], [old[19]]
-        change = jnp.zeros((SUB, LANE), jnp.float32)
-        closed = {}
-        for i in range(1, 19):
-            if rd == 0:
-                word = masks[(i - 1) // 9, r]
-                enabled = ((word >> ((i - 1) % 9)) & 1).astype(jnp.float32)
-                here = kind_from[i]
-                if VELOCITY[i][2] < 0:
-                    here = jnp.where(top, 0.0, here)
-                code[i - 1, r] = here
-                whole = jnp.where(here == 2.0, enabled, 0.0)
-                part = jnp.where(here == 1.0, 0.5 * enabled, 0.0)
-                liquid[i - 1, r] = whole
-                shared[i - 1, r] = part
-            else:
-                here, whole, part = code[i - 1, r], liquid[i - 1, r], shared[i - 1, r]
-            wall, gas = here == 3.0, here == 0.0
-            dx, dy, dz = VELOCITY[i]
-            along = sum(s * u for s, u in zip((dx, dy, dz), (ux, uy, uz)) if s)
-            rebuilt = WEIGHTS[i] * (base + 9.0 * (along * along))
-            arriving, back = incoming(i), old[OPPOSITE[i]]
-            f_new.append(jnp.where(wall, back, jnp.where(gas, rebuilt - back, arriving)))
-            change = change + (whole + part * (frac + frac_from[i])) * (arriving - back)
-            if i < 7:
-                closed[i] = jnp.logical_or(wall, gas)
-        for k in range(1, 7):
-            g_new.append(jnp.where(closed[k], old[19 + OPPOSITE[k]], incoming(19 + k)))
-        fluid = jnp.logical_or(kind == 1, kind == 2)
-        f_new = [jnp.where(fluid, f_new[i], flow[i, r]) for i in range(19)]
-        g_new = [jnp.where(fluid, g_new[k], warm[k, r]) for k in range(7)]
-        total = functools.reduce(jnp.add, f_new)
-        m_new = jnp.where(kind == 1, mass[r] + change, jnp.where(kind == 2, total, 0.0))
+        f_new, g_new, changes = {0: old[0]}, {0: old[19]}, []
+        for directions in stages:
+            yield
+            terms = []
+            for i in directions:
+                if rd == 0:
+                    word = masks[(i - 1) // 9, r]
+                    enabled = ((word >> ((i - 1) % 9)) & 1).astype(jnp.float32)
+                    here = at_source(i, KIND_A, kind.astype(jnp.float32))
+                    if VELOCITY[i][2] < 0:
+                        here = jnp.where(top, 0.0, here)
+                    code[i - 1, r] = here
+                    whole = jnp.where(here == 2.0, enabled, 0.0)
+                    part = jnp.where(here == 1.0, 0.5 * enabled, 0.0)
+                    liquid[i - 1, r] = whole
+                    shared[i - 1, r] = part
+                else:
+                    here, whole, part = code[i - 1, r], liquid[i - 1, r], shared[i - 1, r]
+                wall, gas = here == 3.0, here == 0.0
+                along = sum(s * u for s, u in zip(VELOCITY[i], (ux, uy, uz)) if s)
+                rebuilt = WEIGHTS[i] * (base + 9.0 * (along * along))
+                arriving, back = incoming(i), old[OPPOSITE[i]]
+                f_new[i] = jnp.where(wall, back, jnp.where(gas, rebuilt - back, arriving))
+                terms.append((whole + part * (frac + at_source(i, FRAC, frac))) * (arriving - back))
+                if i < 7:
+                    g_new[i] = jnp.where(jnp.logical_or(wall, gas), old[19 + OPPOSITE[i]], incoming(19 + i))
+            changes.append(tree(terms))
+        f_new = [jnp.where(fluid, f_new[i], state[i, r]) for i in range(19)]
+        g_new = [jnp.where(fluid, g_new[k], state[19 + k, r]) for k in range(7)]
+        m_new = jnp.where(kind == 1, state[MASS, r] + tree(changes), jnp.where(kind == 2, tree(f_new), 0.0))
         if rd == ITERS - 1:
             for i in range(19):
                 flow_out[i, r] = f_new[i]
@@ -338,53 +346,127 @@
                 heat_out[k, r] = g_new[k]
             mass_out[r] = m_new
             return
-        for i in range(19):
-            flow[i, r] = f_new[i]
-        for k in range(7):
-            warm[k, r] = g_new[k]
-        mass[r] = m_new
+        for i, value in enumerate(f_new + g_new + [m_new]):
+            state[i, r] = value
         collide_row(rd + 1, r, f_new, g_new, m_new)
 
     def first_row(r):
-        collide_row(0, r, [flow[i, r] for i in range(19)], [warm[k, r] for k in range(7)], mass[r])
-
-    def wait(copies):
-        for copy in copies:
-            copy.wait()
-
-    def rows_in_turn(body, first, step):
-        lax.fori_loop(0, 2, lambda k, _: (body(first + step * k), 0)[1], 0)
-
-    wait(last_loads)
+        collide_row(0, r, [state[i, r] for i in range(19)], [state[19 + k, r] for k in range(7)], state[MASS, r])
+
+    def whole_rows(rd, first, step):
+        def body(k, _):
+            for _ in stream_row(rd, first + step * k, [range(1, 19)]):
+                pass
+            return 0
+
+        lax.fori_loop(0, 2, body, 0)
+
+    def end_row(rd, r, way):
+        return stream_row(
+            rd,
+            r,
+            [
+                [i for i in range(1, 19) if VELOCITY[i][0] != way and VELOCITY[i][1] == 0],
+                [i for i in range(1, 19) if VELOCITY[i][0] != way and VELOCITY[i][1]],
+                [i for i in range(1, 19) if VELOCITY[i][0] == way],
+            ],
+        )
+
+    def beside_row(rd, r, way):
+        late = [i for i in range(7, 11) if VELOCITY[i][0] == way]
+        return stream_row(rd, r, [[i for i in range(1, 19) if i not in late], late])
+
+    def step_on(*rows):
+        for row in rows:
+            next(row, None)
+
+    wait_rows(ROWS - 1, 1, 0)
+    cells = state.at[pl.ds(MASS, 3)]
+    pltpu.make_async_copy(cells, cells, load_sem.at[5]).wait()
+    load_kinds.wait()
     first_row(ROWS - 1)
-    wait(first_loads)
+    wait_rows(0, 1, 1)
     first_row(0)
+    def first_inner():
+        wait_rows(1, ROWS - 2, 2)
+        lax.fori_loop(1, ROWS - 1, lambda r, _: (first_row(r), 0)[1], 0)
+
+    early = gx % (gx_size // 2) == 0
+    later = jnp.logical_not(early)
+    pl.when(early)(first_inner)
     pl.semaphore_wait(barrier, sum(there(dx, dy).astype(jnp.int32) for dx, dy in NEIGHBOURS))
-    send(0, TO_HIGH + TO_LOW + Y_LOW + Y_HIGH)
-    wait(inner_loads)
-    lax.fori_loop(1, ROWS - 1, lambda r, _: (first_row(r), 0)[1], 0)
-    send(0, Y_INNER)
+
+    @pl.when(early)
+    def _():
+        send(0, TO_LOW, Y_LOW, Y_INNER, Y_HIGH, TO_HIGH)
+
+    @pl.when(later)
+    def _():
+        send(0, TO_HIGH, TO_LOW, Y_HIGH, Y_LOW)
+        first_inner()
+        send(0, Y_INNER)
+
+    load_masks.wait()
     for rd in range(ITERS):
-        more = rd < ITERS - 1
-        receive(rd, Y_INNER)
-        rows_in_turn(lambda r: stream_row(rd, r, False), 2, 1)
-        ends = [(0, 1, TO_HIGH + Y_LOW, TO_LOW + Y_LOW), (ROWS - 1, ROWS - 2, TO_LOW + Y_HIGH, TO_HIGH + Y_HIGH)]
-        for r, beside, needed, leaving in ends if more else reversed(ends):
-            receive(rd, needed)
-            stream_row(rd, r, r == ROWS - 1)
-            if more:
-                send(rd + 1, leaving)
-            else:
-                stream_row(rd, beside, False)
-        if more:
-            rows_in_turn(lambda r: stream_row(rd, r, False), 1, ROWS - 3)
+        inner_pair = functools.partial(whole_rows, rd, 2, 1)
+
+        def outer_pair():
+            whole_rows(rd, 1, ROWS - 3)
             send(rd + 1, Y_INNER)
-    for cls in range(len(CLASSES)):
-
-        @pl.when(there(*CLASSES[cls][:2]))
-        def _():
-            for rd in range(ITERS):
-                copy_of(rd, cls).wait_send()
+
+        def end(r, way, across, leaving, wait_along):
+            row = end_row(rd, r, way)
+            step_on(row, row)
+            wait_along()
+            step_on(row)
+            receive(rd, across)
+            step_on(row)
+            send(rd + 1, *leaving)
+
+        if rd == 0:
+
+            @pl.when(later)
+            def _():
+                receive(rd, Y_INNER)
+                inner_pair()
+                receive(rd, Y_LOW, Y_HIGH)
+                outer_pair()
+
+            end(
+                0, 1, TO_HIGH, (TO_LOW, Y_LOW), lambda: pl.when(early)(lambda: receive(rd, Y_INNER, Y_LOW, Y_HIGH))
+            )
+
+            @pl.when(early)
+            def _():
+                inner_pair()
+                outer_pair()
+
+            end(ROWS - 1, -1, TO_LOW, (Y_HIGH, TO_HIGH), lambda: None)
+        elif rd < ITERS - 1:
+            receive(rd, Y_INNER)
+            inner_pair()
+            drain(rd - 1)
+
+            @pl.when(early)
+            def _():
+                receive(rd, Y_LOW, Y_HIGH)
+                outer_pair()
+
+            end(0, 1, TO_HIGH, (Y_LOW, TO_LOW), lambda: pl.when(later)(lambda: receive(rd, Y_LOW)))
+            end(ROWS - 1, -1, TO_LOW, (TO_HIGH, Y_HIGH), lambda: pl.when(later)(lambda: receive(rd, Y_HIGH)))
+            pl.when(later)(outer_pair)
+        else:
+            receive(rd, Y_INNER)
+            inner_pair()
+            drain(rd - 1)
+            drain(rd)
+            for r, way, across, along in ((ROWS - 1, -1, TO_LOW, Y_HIGH), (0, 1, TO_HIGH, Y_LOW)):
+                row, beside = end_row(rd, r, way), beside_row(rd, r + way, way)
+                step_on(row, row, beside, beside)
+                receive(rd, along)
+                step_on(beside, row)
+                receive(rd, across)
+                step_on(row)
 
 
 def write_out(*refs):
@@ -412,11 +494,7 @@
             in_specs=[in_hbm] * 7,
             out_specs=[in_vmem] * 3,
             scratch_shapes=[
-                pltpu.VMEM((19,) + row, f32),
-                pltpu.VMEM((7,) + row, f32),
-                pltpu.VMEM(row, f32),
-                pltpu.VMEM(row, f32),
-                pltpu.VMEM(row, f32),
+                pltpu.VMEM((29,) + row, f32),
                 pltpu.VMEM(row, i32),
                 pltpu.VMEM((2,) + row, i32),
                 pltpu.VMEM((26,) + row, f32),
@@ -428,9 +506,10 @@
                 pltpu.VMEM((18,) + row, f32),
                 pltpu.VMEM((18,) + row, f32),
                 pltpu.VMEM((18,) + row, f32),
-                pltpu.SemaphoreType.DMA((11,)),
-                pltpu.SemaphoreType.DMA((ITERS, len(CLASSES))),
-                pltpu.SemaphoreType.DMA((ITERS, len(CLASSES))),
+                pltpu.VMEM((72, LANE), f32),
+                pltpu.SemaphoreType.DMA((6,)),
+                pltpu.SemaphoreType.DMA((2, len(GROUPS))),
+                pltpu.SemaphoreType.DMA((2, len(GROUPS))),
             ],
             compiler_params=pltpu.CompilerParams(
                 collective_id=0, has_side_effects=True, vmem_limit_bytes=24 * 1024 * 1024

time: 27.6 us -> 26.4 us (0.957)
  Pallas kernels: 26.8 us -> 25.6 us
    pallas_call x1, Pallas kernels: 25.9 us -> 24.8 us  [shards(): pl.pallas_call(functools.partial(kernel, gx_size, gy_size), out_shape=[pl...]
where the time goes in v3:
time: 26.4 us; the launch traced here: 26.3 us
  Pallas kernels  25.6 us (97%)
  between operations  0.64 us (2%)
    pallas_call x1, Pallas kernels, shards(): pl.pallas_call(functools.partial(kernel, gx_size, gy_size), out_shape=[pl...  24.8 us
    pallas_call x1, Pallas kernels, shards(): pl.pallas_call(write_out, out_shape=[jax.ShapeDtypeStruct(s, f32) for s i...  0.85 us

profile of v3, /device:TPU:7, one launch (start us, length us, event | category | flops | bytes accessed | tf_op | source)
XLA Modules:
  0.0 26.3 jit_solution(12940263751673056771)
XLA Ops:
  0.6 24.8 %shard_map.94 = (f32[19,6,8,128]{3,2,1,0:T(8,128)S(1)}, f32[7,6,8,128]{3,2,1,0:T(8,128)S(1)}, f32[6,8,128]{2,1,0:T(8,128)S(1)}) custom-call(f32[19,6,8,128]{3,2,1,0:T(8,128)} %refs_0_.1, f32[7,6,8,128]{3,2,1,0:T(8,128)} %refs_1_.1, f32[6,8,128]{2,1,0:T(8,128)} %refs_2_.1, f32[6,8,128]{2,1,0:T(8,128)} %refs_3_.1, f32[6,8,128]{2,1,0:T(8,128)} %refs_4_.1, ...), custom_call_target="tpu_custom_call" | custom-call | tf_op jit(solution)/shard_map/pallas_call | solution.py:491
  25.4 0.9 %shard_map.95 = (f32[19,6,8,128]{3,2,1,0:T(8,128)}, f32[7,6,8,128]{3,2,1,0:T(8,128)}, f32[6,8,128]{2,1,0:T(8,128)}) custom-call(f32[19,6,8,128]{3,2,1,0:T(8,128)S(1)} %get-tuple-element.6.refs_0_, f32[7,6,8,128]{3,2,1,0:T(8,128)S(1)} %get-tuple-element.7.refs_1_, f32[6,8,128]{2,1,0:T(8,128)S(1)} %get-tuple-element.8.refs_2_), custom_call_target="tpu_custom_call" | custom-call | tf_op jit(solution)/shard_map/pallas_call | solution.py:520

commit v4 on v3

--- a/solution.py
+++ b/solution.py
@@ -150,11 +150,15 @@
         return functools.reduce(jnp.logical_and, tests)
 
     barrier = pltpu.get_barrier_semaphore()
-    for dx, dy in NEIGHBOURS:
-
-        @pl.when(there(dx, dy))
-        def _():
-            pl.semaphore_signal(barrier, inc=1, device_id=(gx + dx, gy + dy), device_id_type=MESH)
+
+    def greet(ways):
+        for dx, dy in ways:
+
+            @pl.when(there(dx, dy))
+            def _():
+                pl.semaphore_signal(barrier, inc=1, device_id=(gx + dx, gy + dy), device_id_type=MESH)
+
+    greet([way for way in NEIGHBOURS if way[0] > 0])
 
     def rows_of(at, size, sem):
         rows = pl.ds(at, size)
@@ -168,14 +172,16 @@
         pltpu.make_async_copy(there, there, load_sem.at[sem]).wait()
 
     load_kinds = pltpu.make_async_copy(kind_in, kinds, load_sem.at[3])
-    load_masks = pltpu.make_async_copy(mask_in, masks, load_sem.at[4])
+    load_masks = pltpu.make_async_copy(mask_in, masks, load_sem.at[3])
     load_cells = [
-        pltpu.make_async_copy(src, state.at[at], load_sem.at[5])
+        pltpu.make_async_copy(src, state.at[at], load_sem.at[0])
         for src, at in ((mass_in, MASS), (diff_in, RATE), (source_in, SOURCE))
     ]
-    for load in rows_of(ROWS - 1, 1, 0) + load_cells + [load_kinds] + rows_of(0, 1, 1) + rows_of(1, ROWS - 2, 2):
+    for load in rows_of(ROWS - 1, 1, 0) + load_cells + [load_kinds]:
         load.start()
-    load_masks.start()
+    greet([way for way in NEIGHBOURS if way[0] <= 0])
+    for load in rows_of(0, 1, 1) + rows_of(1, ROWS - 2, 2):
+        load.start()
 
     def copy_of(rd, cls):
         dx, dy, part = CLASSES[cls]
@@ -204,7 +210,7 @@
         return pltpu.make_async_remote_copy(
             src_ref=src,
             dst_ref=dst,
-            send_sem=send_sem.at[rd % 2, group],
+            send_sem=send_sem.at[rd % 2],
             recv_sem=recv_sem.at[rd % 2, group],
             device_id=(gx + dx, gy + dy),
             device_id_type=MESH,
@@ -218,21 +224,27 @@
                 def _():
                     copy_of(rd, cls).start()
 
+    def wait_lines(test, count, sem):
+        @pl.when(test)
+        def _():
+            lines = t_size.at[pl.ds(0, count)]
+            pltpu.make_async_copy(lines, lines, sem).wait()
+
+    inside_x = jnp.logical_and(gx > 0, gx < gx_size - 1)
+    inside_y = jnp.logical_and(gy > 0, gy < gy_size - 1)
+
     def wait_group(rd, group, sem, there_x):
         fields = 8 if rd == 0 else 7
         fixed, each = (fields * SUB, fields - 5) if group < 2 else (0, fields * CLASSES[GROUPS[group][0]][2][1])
-        inside = jnp.logical_and(gy > 0, gy < gy_size - 1)
-        for both in (True, False):
-            test = inside if both else jnp.logical_not(inside)
-
-            @pl.when(jnp.logical_and(test, there_x) if group < 2 else test)
-            def _():
-                lines = t_size.at[pl.ds(0, fixed + each * (2 if both else 1))]
-                pltpu.make_async_copy(lines, lines, sem).wait()
+        for sides, test in ((2, inside_y), (1, jnp.logical_not(inside_y))):
+            wait_lines(jnp.logical_and(test, there_x) if group < 2 else test, fixed + each * sides, sem)
 
     def drain(rd):
-        for group in range(len(GROUPS)):
-            wait_group(rd, group, send_sem.at[rd % 2, group], there(CLASSES[GROUPS[group][0]][0], 0) if group < 2 else None)
+        fields = 8 if rd == 0 else 7
+        for sides_x, test_x in ((2, inside_x), (1, jnp.logical_not(inside_x))):
+            for sides_y, test_y in ((2, inside_y), (1, jnp.logical_not(inside_y))):
+                count = sides_x * (fields * SUB + sides_y * (fields - 5)) + sides_y * fields * ROWS
+                wait_lines(jnp.logical_and(test_x, test_y), count, send_sem.at[rd % 2])
 
     def receive(rd, *groups):
         for group in groups:
@@ -361,13 +373,16 @@
 
         lax.fori_loop(0, 2, body, 0)
 
-    def end_row(rd, r, way):
+    def end_row(rd, r, way, inner_there=True):
+        here = [i for i in range(1, 19) if VELOCITY[i][0] != way and VELOCITY[i][1] == 0]
+        if inner_there:
+            here += [i for i in range(7, 11) if VELOCITY[i][0] == -way]
         return stream_row(
             rd,
             r,
             [
-                [i for i in range(1, 19) if VELOCITY[i][0] != way and VELOCITY[i][1] == 0],
-                [i for i in range(1, 19) if VELOCITY[i][0] != way and VELOCITY[i][1]],
+                here,
+                [i for i in range(1, 19) if VELOCITY[i][0] != way and i not in here],
                 [i for i in range(1, 19) if VELOCITY[i][0] == way],
             ],
         )
@@ -380,20 +395,28 @@
         for row in rows:
             next(row, None)
 
-    wait_rows(ROWS - 1, 1, 0)
-    cells = state.at[pl.ds(MASS, 3)]
-    pltpu.make_async_copy(cells, cells, load_sem.at[5]).wait()
+    lines = t_size.at[pl.ds(0, 26 * SUB + 3 * ROWS * SUB)]
+    pltpu.make_async_copy(lines, lines, load_sem.at[0]).wait()
     load_kinds.wait()
+    load_masks.start()
     first_row(ROWS - 1)
-    wait_rows(0, 1, 1)
-    first_row(0)
+
+    def first_low():
+        wait_rows(0, 1, 1)
+        first_row(0)
+
     def first_inner():
         wait_rows(1, ROWS - 2, 2)
         lax.fori_loop(1, ROWS - 1, lambda r, _: (first_row(r), 0)[1], 0)
 
     early = gx % (gx_size // 2) == 0
     later = jnp.logical_not(early)
-    pl.when(early)(first_inner)
+
+    @pl.when(early)
+    def _():
+        first_low()
+        first_inner()
+
     pl.semaphore_wait(barrier, sum(there(dx, dy).astype(jnp.int32) for dx, dy in NEIGHBOURS))
 
     @pl.when(early)
@@ -402,7 +425,9 @@
 
     @pl.when(later)
     def _():
-        send(0, TO_HIGH, TO_LOW, Y_HIGH, Y_LOW)
+        send(0, TO_HIGH, Y_HIGH)
+        first_low()
+        send(0, TO_LOW, Y_LOW)
         first_inner()
         send(0, Y_INNER)
 
@@ -415,7 +440,7 @@
             send(rd + 1, Y_INNER)
 
         def end(r, way, across, leaving, wait_along):
-            row = end_row(rd, r, way)
+            row = end_row(rd, r, way, rd > 0 or r > 0)
             step_on(row, row)
             wait_along()
             step_on(row)
@@ -433,12 +458,13 @@
                 outer_pair()
 
             end(
-                0, 1, TO_HIGH, (TO_LOW, Y_LOW), lambda: pl.when(early)(lambda: receive(rd, Y_INNER, Y_LOW, Y_HIGH))
+                0, 1, TO_HIGH, (TO_LOW, Y_LOW), lambda: pl.when(early)(lambda: receive(rd, Y_INNER, Y_LOW))
             )
 
             @pl.when(early)
             def _():
                 inner_pair()
+                receive(rd, Y_HIGH)
                 outer_pair()
 
             end(ROWS - 1, -1, TO_LOW, (Y_HIGH, TO_HIGH), lambda: None)
@@ -506,9 +532,9 @@
                 pltpu.VMEM((18,) + row, f32),
                 pltpu.VMEM((18,) + row, f32),
                 pltpu.VMEM((18,) + row, f32),
-                pltpu.VMEM((72, LANE), f32),
-                pltpu.SemaphoreType.DMA((6,)),
-                pltpu.SemaphoreType.DMA((2, len(GROUPS))),
+                pltpu.VMEM((352, LANE), f32),
+                pltpu.SemaphoreType.DMA((4,)),
+                pltpu.SemaphoreType.DMA((2,)),
                 pltpu.SemaphoreType.DMA((2, len(GROUPS))),
             ],
             compiler_params=pltpu.CompilerParams(

time: 26.4 us -> 26.3 us (level)
  no operation moved by 1% of the time
where the time goes in v4:
time: 26.3 us; the launch traced here: 26.1 us
  Pallas kernels  25.5 us (97%)
  between operations  0.64 us (2%)
    pallas_call x1, Pallas kernels, shards(): pl.pallas_call(functools.partial(kernel, gx_size, gy_size), out_shape=[pl...  24.6 us
    pallas_call x1, Pallas kernels, shards(): pl.pallas_call(write_out, out_shape=[jax.ShapeDtypeStruct(s, f32) for s i...  0.85 us

profile of v4, /device:TPU:7, one launch (start us, length us, event | category | flops | bytes accessed | tf_op | source)
XLA Modules:
  0.0 26.1 jit_solution(17163966091749099970)
XLA Ops:
  0.6 24.6 %shard_map.94 = (f32[19,6,8,128]{3,2,1,0:T(8,128)S(1)}, f32[7,6,8,128]{3,2,1,0:T(8,128)S(1)}, f32[6,8,128]{2,1,0:T(8,128)S(1)}) custom-call(f32[19,6,8,128]{3,2,1,0:T(8,128)} %refs_0_.1, f32[7,6,8,128]{3,2,1,0:T(8,128)} %refs_1_.1, f32[6,8,128]{2,1,0:T(8,128)} %refs_2_.1, f32[6,8,128]{2,1,0:T(8,128)} %refs_3_.1, f32[6,8,128]{2,1,0:T(8,128)} %refs_4_.1, ...), custom_call_target="tpu_custom_call" | custom-call | tf_op jit(solution)/shard_map/pallas_call | solution.py:517
  25.2 0.9 %shard_map.95 = (f32[19,6,8,128]{3,2,1,0:T(8,128)}, f32[7,6,8,128]{3,2,1,0:T(8,128)}, f32[6,8,128]{2,1,0:T(8,128)}) custom-call(f32[19,6,8,128]{3,2,1,0:T(8,128)S(1)} %get-tuple-element.6.refs_0_, f32[7,6,8,128]{3,2,1,0:T(8,128)S(1)} %get-tuple-element.7.refs_1_, f32[6,8,128]{2,1,0:T(8,128)S(1)} %get-tuple-element.8.refs_2_), custom_call_target="tpu_custom_call" | custom-call | tf_op jit(solution)/shard_map/pallas_call | solution.py:546

commit v5 on v4

--- a/solution.py
+++ b/solution.py
@@ -47,7 +47,7 @@
 ]
 NEIGHBOURS = [(1, 0), (-1, 0), (1, 1), (1, -1), (-1, 1), (-1, -1), (0, 1), (0, -1)]
 LOW, HIGH, INNER = (1, 1), (ROWS, 1), (2, ROWS - 2)
-CLASSES = [way + (None,) for way in NEIGHBOURS[:6]] + [(0, dy, part) for part in (LOW, HIGH, INNER) for dy in (1, -1)]
+CLASSES = [way + (None,) for way in NEIGHBOURS[:6]] + [(0, dy, part) for part in (LOW, HIGH, INNER) for dy in (-1, 1)]
 GROUPS = [(0, 2, 3), (1, 4, 5), (6, 7), (8, 9), (10, 11)]
 TO_HIGH, TO_LOW, Y_LOW, Y_HIGH, Y_INNER = range(5)
 
@@ -467,7 +467,7 @@
                 receive(rd, Y_HIGH)
                 outer_pair()
 
-            end(ROWS - 1, -1, TO_LOW, (Y_HIGH, TO_HIGH), lambda: None)
+            end(ROWS - 1, -1, TO_LOW, (TO_HIGH, Y_HIGH), lambda: None)
         elif rd < ITERS - 1:
             receive(rd, Y_INNER)
             inner_pair()
@@ -477,10 +477,14 @@
             def _():
                 receive(rd, Y_LOW, Y_HIGH)
                 outer_pair()
+                end(ROWS - 1, -1, TO_LOW, (Y_HIGH, TO_HIGH), lambda: None)
 
             end(0, 1, TO_HIGH, (Y_LOW, TO_LOW), lambda: pl.when(later)(lambda: receive(rd, Y_LOW)))
-            end(ROWS - 1, -1, TO_LOW, (TO_HIGH, Y_HIGH), lambda: pl.when(later)(lambda: receive(rd, Y_HIGH)))
-            pl.when(later)(outer_pair)
+
+            @pl.when(later)
+            def _():
+                end(ROWS - 1, -1, TO_LOW, (TO_HIGH, Y_HIGH), lambda: receive(rd, Y_HIGH))
+                outer_pair()
         else:
             receive(rd, Y_INNER)
             inner_pair()

time: 26.3 us -> 26.3 us (level)
  no operation moved by 1% of the time
where the time goes in v5:
time: 26.3 us; the launch traced here: 26.1 us
  Pallas kernels  25.4 us (97%)
  between operations  0.64 us (2%)
    pallas_call x1, Pallas kernels, shards(): pl.pallas_call(functools.partial(kernel, gx_size, gy_size), out_shape=[pl...  24.6 us
    pallas_call x1, Pallas kernels, shards(): pl.pallas_call(write_out, out_shape=[jax.ShapeDtypeStruct(s, f32) for s i...  0.85 us

profile of v5, /device:TPU:7, one launch (start us, length us, event | category | flops | bytes accessed | tf_op | source)
XLA Modules:
  0.0 26.1 jit_solution(15716894678294585638)
XLA Ops:
  0.6 24.6 %shard_map.94 = (f32[19,6,8,128]{3,2,1,0:T(8,128)S(1)}, f32[7,6,8,128]{3,2,1,0:T(8,128)S(1)}, f32[6,8,128]{2,1,0:T(8,128)S(1)}) custom-call(f32[19,6,8,128]{3,2,1,0:T(8,128)} %refs_0_.1, f32[7,6,8,128]{3,2,1,0:T(8,128)} %refs_1_.1, f32[6,8,128]{2,1,0:T(8,128)} %refs_2_.1, f32[6,8,128]{2,1,0:T(8,128)} %refs_3_.1, f32[6,8,128]{2,1,0:T(8,128)} %refs_4_.1, ...), custom_call_target="tpu_custom_call" | custom-call | tf_op jit(solution)/shard_map/pallas_call | solution.py:521
  25.2 0.9 %shard_map.95 = (f32[19,6,8,128]{3,2,1,0:T(8,128)}, f32[7,6,8,128]{3,2,1,0:T(8,128)}, f32[6,8,128]{2,1,0:T(8,128)}) custom-call(f32[19,6,8,128]{3,2,1,0:T(8,128)S(1)} %get-tuple-element.6.refs_0_, f32[7,6,8,128]{3,2,1,0:T(8,128)S(1)} %get-tuple-element.7.refs_1_, f32[6,8,128]{2,1,0:T(8,128)S(1)} %get-tuple-element.8.refs_2_), custom_call_target="tpu_custom_call" | custom-call | tf_op jit(solution)/shard_map/pallas_call | solution.py:550
